TPU v7x, 32 devices: a whole 2x2x4 slice. The times are simulated.
32 devices in a mesh: cfg: 2 (over x), req: 4 (over z), seq: 4 (over y, core).
Axes of the slice: x: 2, y: 2, z: 4, core: 2. Of those that a mesh axis runs over, the one named last changes fastest.
Arguments:
- img_state: bfloat16 [2, 8, 1024, 1536], P('cfg', 'req', 'seq'), may hold values from -6 to 6
- txt_state: bfloat16 [2, 8, 192, 1536], P('cfg', 'req', 'seq'), may hold values from -6 to 6
- cond_vec: float32 [2, 8, 1536], P('cfg'), may hold values from -6 to 6
- text_len: int32 [2, 8], P('cfg', 'req'), may hold values from 38 to 154, as said below
- latent: float32 [8, 1024, 64], P('req', 'seq', 'cfg'), may hold values from -6 to 6
- w_mod: bfloat16 [15360, 1536], P(('req', 'seq')), may hold values from -0.15625 to 0.15625
- w_qkv_img: bfloat16 [3, 1536, 1536], P(None, 'seq')
- w_qkv_txt: bfloat16 [3, 1536, 1536], P(None, 'seq')
- w_attn_out: bfloat16 [1536, 1536], P('seq'), may hold values from -2 to 2
- w_up: bfloat16 [6144, 1536], P(('cfg', 'req', 'seq')), may hold values from -0.15625 to 0.15625
- w_down: bfloat16 [6144, 1536], P(('cfg', 'req', 'seq')), may hold values from -0.078125 to 0.078125
- w_final: bfloat16 [1536, 64], replicated, may hold values from -0.078125 to 0.078125
Outputs:
- velocity: float32 [8, 1024, 64], P('req', 'seq', 'cfg')
- latent_next: float32 [8, 1024, 64], P('req', 'seq', 'cfg')
Inputs may be any that keep to these rules, and one draw needn't show every extreme that they name: Text slot t of prompt p in branch c is live when t < text_len[c, p]; every draw has a length equal to 154.
All inputs are finite; a program needn't handle non-finite values.
Results may differ from a plain program's by a relative error of at most 0.02.
Values may be sent and summed in bfloat16 or wider, within the bound.
A program may use at most 128 MiB of HBM per device.

v0:
```python
import functools

import jax
import jax.numpy as jnp
from jax import lax
from jax.experimental import pallas as pl
from jax.experimental.pallas import tpu as pltpu
from jax.sharding import PartitionSpec as P

HEAD = 64
VMEM_BYTES = 56 * 1024 * 1024


def partner_2(shard, axis, apart):
    return lax.ppermute(shard, axis, [(i, i ^ 1 << apart) for i in range(lax.axis_size(axis))])


def layer_norm(value):
    mean = jnp.mean(value, axis=-1, keepdims=True)
    centered = value - mean
    spread = jnp.mean(centered * centered, axis=-1, keepdims=True)
    return centered * lax.rsqrt(spread + 1e-06)


def mlp_term(rows_in, up_block, down_block):
    inner = lax.dot_general(
        rows_in, up_block, (((1,), (1,)), ((), ())), preferred_element_type=jnp.float32
    )
    hidden = jax.nn.gelu(inner, approximate=True).astype(jnp.bfloat16)
    return jnp.dot(hidden, down_block, preferred_element_type=jnp.float32)


def local(
    img_state,
    txt_state,
    cond_vec,
    text_len,
    latent,
    w_mod,
    w_qkv_img,
    w_qkv_txt,
    w_attn_out,
    w_up,
    w_down,
    w_final,
):
    prompts_dev = img_state.shape[1]
    img_rows = img_state.shape[2]
    width = img_state.shape[3]
    cond_act = jax.nn.silu(cond_vec[0]).astype(jnp.bfloat16)
    mod_part = lax.dot_general(
        cond_act, w_mod, (((1,), (1,)), ((), ())), preferred_element_type=jnp.float32
    )
    mod_all = lax.all_gather(mod_part, ("req", "seq"), axis=1, tiled=True)
    mine = lax.dynamic_slice_in_dim(mod_all, lax.axis_index("req") * prompts_dev, prompts_dev, 0)
    parts = mine.reshape(prompts_dev, 10, 1, width)
    resid = img_state[0].astype(jnp.float32)
    a_img = (layer_norm(resid) * (1.0 + parts[:, 1]) + parts[:, 0]).astype(jnp.bfloat16)
    a_txt = (
        layer_norm(txt_state[0].astype(jnp.float32)) * (1.0 + parts[:, 7]) + parts[:, 6]
    ).astype(jnp.bfloat16)
    full_img, full_txt = (
        lax.all_gather(a_img, "seq", axis=1, tiled=True),
        lax.all_gather(a_txt, "seq", axis=1, tiled=True),
    )
    proj_img = jnp.einsum(
        "pnd,jed->jpne", full_img, w_qkv_img, preferred_element_type=jnp.float32
    ).astype(jnp.bfloat16)
    proj_txt = jnp.einsum(
        "pnd,jed->jpne", full_txt, w_qkv_txt, preferred_element_type=jnp.float32
    ).astype(jnp.bfloat16)
    total_img = full_img.shape[1]
    local_width = w_qkv_img.shape[1]
    heads_local = local_width // HEAD
    key_heads = jnp.concatenate([proj_img[1], proj_txt[1]], axis=1).reshape(
        prompts_dev, -1, heads_local, HEAD
    )
    value_heads = jnp.concatenate([proj_img[2], proj_txt[2]], axis=1).reshape(
        prompts_dev, -1, heads_local, HEAD
    )
    live = jnp.arange(key_heads.shape[1])[None, :] < (total_img + text_len[0])[:, None]
    block = min(512, total_img)
    queries = proj_img[0].reshape(prompts_dev, total_img // block, block, heads_local, HEAD)

    def attend(query):
        scores = jnp.einsum(
            "pqhe,pkhe->phqk", query, key_heads, preferred_element_type=jnp.float32
        ) * HEAD ** (-0.5)
        scores = jnp.where(live[:, None, None, :], scores, -1e30)
        probs = jax.nn.softmax(scores, axis=-1).astype(jnp.bfloat16)
        return jnp.einsum(
            "phqk,pkhe->pqhe", probs, value_heads, preferred_element_type=jnp.float32
        ).astype(jnp.bfloat16)

    attended = lax.map(attend, jnp.moveaxis(queries, 1, 0))
    attended = jnp.moveaxis(attended, 0, 1).reshape(prompts_dev, total_img, local_width)
    proj = jnp.swapaxes(
        lax.psum_scatter(
            jnp.einsum(
                "pnh,hd->npd", attended, w_attn_out, preferred_element_type=jnp.float32
            ).astype(jnp.bfloat16),
            "seq",
            scatter_dimension=0,
            tiled=True,
        ).astype(jnp.float32),
        0,
        1,
    )
    resid_one = (resid + parts[:, 2] * proj).astype(jnp.bfloat16)
    normed = (layer_norm(resid_one.astype(jnp.float32)) * (1.0 + parts[:, 4]) + parts[:, 3]).astype(
        jnp.bfloat16
    )
    own_rows = normed.reshape(prompts_dev * img_rows, width)
    both = lax.all_gather(own_rows, "cfg", axis=0, tiled=True)
    partial_out = mlp_term(
        both,
        lax.all_gather(w_up, ("req", "seq"), axis=0, tiled=True),
        lax.all_gather(w_down, ("req", "seq"), axis=0, tiled=True),
    )
    mlp_out = lax.psum_scatter(
        partial_out.astype(jnp.bfloat16), "cfg", scatter_dimension=0, tiled=True
    ).astype(jnp.float32)
    mlp_out = mlp_out.reshape(prompts_dev, img_rows, width)
    resid_two = resid_one.astype(jnp.float32) + parts[:, 5] * mlp_out
    final_in = (layer_norm(resid_two) * (1.0 + parts[:, 9]) + parts[:, 8]).astype(jnp.bfloat16)
    branch_vel = jnp.einsum("pnd,dc->pnc", final_in, w_final, preferred_element_type=jnp.float32)
    return guide(branch_vel, latent)

def flip(shard, bits, axis="seq"):
    return lax.ppermute(shard, axis, [(i, i ^ bits) for i in range(lax.axis_size(axis))])


def after(value, first):
    return lax.optimization_barrier((value, first))[0]


def norm_rows(rows, scale, shift):
    return (layer_norm(rows.astype(jnp.float32)) * (1.0 + scale) + shift).astype(jnp.bfloat16)


def across(left, right):
    return lax.dot_general(
        left, right, (((1,), (1,)), ((), ())), preferred_element_type=jnp.float32
    )


def mod_kernel(cond, weight, out, part, got, send_sem, recv_sem):
    reqs, seqs = lax.axis_size("req"), lax.axis_size("seq")
    group = reqs * seqs
    cfg, req = lax.axis_index("cfg"), lax.axis_index("req")
    me = req * seqs + lax.axis_index("seq")
    prompts = part.shape[1]
    barrier = pltpu.get_barrier_semaphore()
    for apart in range(1, group):
        peer = lax.rem(me + apart, group)
        pl.semaphore_signal(
            barrier,
            inc=1,
            device_id=(cfg, peer // seqs, lax.rem(peer, seqs)),
            device_id_type=pl.DeviceIdType.MESH,
        )
    rows = across(jax.nn.silu(cond[...]).astype(jnp.bfloat16), weight[...])
    for at in range(reqs):
        part[at] = rows[at * prompts : (at + 1) * prompts]
    pl.semaphore_wait(barrier, group - 1)
    copies = []
    for apart in range(1, group):
        peer = lax.rem(me + apart, group)
        copy = pltpu.make_async_remote_copy(
            src_ref=part.at[peer // seqs],
            dst_ref=got.at[me],
            send_sem=send_sem.at[apart],
            recv_sem=recv_sem.at[apart],
            device_id=(cfg, peer // seqs, lax.rem(peer, seqs)),
            device_id_type=pl.DeviceIdType.MESH,
        )
        copy.start()
        copies.append(copy)
    got[me] = part[req]
    for copy in copies:
        copy.wait()
    out[...] = got[...]


def modulation(cond, weight):
    reqs, seqs = lax.axis_size("req"), lax.axis_size("seq")
    group, prompts, columns = reqs * seqs, cond.shape[0] // reqs, weight.shape[0]
    vmem = pl.BlockSpec(memory_space=pltpu.VMEM)
    got = pl.pallas_call(
        mod_kernel,
        out_shape=jax.ShapeDtypeStruct((group, prompts, columns), jnp.float32),
        in_specs=[vmem, vmem],
        out_specs=vmem,
        scratch_shapes=[
            pltpu.VMEM((reqs, prompts, columns), jnp.float32),
            pltpu.VMEM((group, prompts, columns), jnp.float32),
            pltpu.SemaphoreType.DMA((group,)),
            pltpu.SemaphoreType.DMA((group,)),
        ],
        compiler_params=pltpu.CompilerParams(
            collective_id=0, has_side_effects=True, vmem_limit_bytes=VMEM_BYTES
        ),
        cost_estimate=pl.CostEstimate(
            flops=2 * cond.size * columns, bytes_accessed=2 * weight.size, transcendentals=0
        ),
    )(cond, weight)
    return jnp.swapaxes(got, 0, 1).reshape(prompts, 10, -1)


def qkv_kernel(owners, img_rows, txt_rows, *refs):
    count = len(owners)
    pieces = refs[:count]
    mod, w_img, w_txt, img_out, txt_out, txt_in = refs[count:]
    for at, (piece, owner) in enumerate(zip(pieces, owners)):
        img = norm_rows(piece[:img_rows], mod[owner, 1:2], mod[owner, 0:1])
        img_out[pl.ds(at * img_rows, img_rows)] = across(img, w_img[...]).astype(jnp.bfloat16)
        txt_in[pl.ds(at * txt_rows, txt_rows)] = norm_rows(
            piece[img_rows:], mod[owner, 7:8], mod[owner, 6:7]
        )
    txt_out[...] = across(txt_in[...], w_txt[...]).astype(jnp.bfloat16)


def project(pieces, owners, img_rows, parts, w_img, w_txt):
    count = len(pieces)
    txt_rows = pieces[0].shape[0] - img_rows
    width = pieces[0].shape[1]
    out = w_img.shape[0]
    rows = count * (img_rows + txt_rows)
    return pl.pallas_call(
        functools.partial(qkv_kernel, owners, img_rows, txt_rows),
        out_shape=(
            jax.ShapeDtypeStruct((count * img_rows, out), jnp.bfloat16),
            jax.ShapeDtypeStruct((count * txt_rows, out), jnp.bfloat16),
        ),
        in_specs=[pl.BlockSpec(memory_space=pltpu.VMEM)] * (count + 3),
        out_specs=(pl.BlockSpec(memory_space=pltpu.VMEM),) * 2,
        scratch_shapes=[pltpu.VMEM((count * txt_rows, width), jnp.bfloat16)],
        compiler_params=pltpu.CompilerParams(vmem_limit_bytes=VMEM_BYTES),
        cost_estimate=pl.CostEstimate(
            flops=2 * rows * width * out, bytes_accessed=4 * out * width, transcendentals=0
        ),
    )(*pieces, parts, w_img, w_txt)


def attend_kernel(
    txt_rows, prompt, length, starts, qa, qb, ka, kb, va, vb, tka, tkb, tva, tvb, out
):
    first = lax.broadcasted_iota(jnp.int32, (1, 2 * HEAD), 1) < HEAD
    column = lax.broadcasted_iota(jnp.int32, (1, 2 * txt_rows), 1)
    live = []
    for base in (0, 2):
        slot = jnp.where(
            column < txt_rows, starts[base] + column, starts[base + 1] + column - txt_rows
        )
        live.append(slot < length[prompt])
    keys = (ka[...], kb[...], tka[...], tkb[...])
    values = (va[...], vb[...], tva[...], tvb[...])
    one = jnp.ones((), jnp.bfloat16)
    zero = jnp.zeros((), jnp.bfloat16)
    held = [
        [jnp.where(first, value, one) for value in values],
        [jnp.where(first, one, value) for value in values],
    ]
    for side, q_ref in enumerate((qa, qb)):
        query = q_ref[...] * jnp.asarray(HEAD ** (-0.5), jnp.bfloat16)
        sums = []
        for head in range(2):
            masked = jnp.where(first, query, zero) if head == 0 else jnp.where(first, zero, query)
            scores = [across(masked, key) for key in keys]
            for text in range(2):
                scores[2 + text] = jnp.where(live[text], scores[2 + text], -1e30)
            top = functools.reduce(
                jnp.maximum, [jnp.max(score, axis=-1, keepdims=True) for score in scores]
            )
            total = None
            for score, value in zip(scores, held[head]):
                weight = jnp.exp(score - top).astype(jnp.bfloat16)
                term = jnp.dot(weight, value, preferred_element_type=jnp.float32)
                total = term if total is None else total + term
            sums.append(total)
        out[0, side] = jnp.where(
            first, sums[0] / sums[0][:, HEAD : HEAD + 1], sums[1] / sums[1][:, 0:1]
        ).astype(jnp.bfloat16)


def attention(prompt, length, starts, near, far, img_rows):
    img_near, txt_near = near
    img_far, txt_far = far
    lanes = 2 * HEAD
    pairs = img_near.shape[1] // (3 * lanes)
    txt_rows = txt_far.shape[0] // 2
    half = 2 * img_rows
    smem = pl.BlockSpec(memory_space=pltpu.SMEM)

    def spec(rows, row_of, third):
        return pl.BlockSpec((rows, lanes), lambda j, i: (row_of(i), third * pairs + j))

    specs = [smem, smem]
    specs += [spec(img_rows, lambda i: 2 * prompt + i, 0), spec(img_rows, lambda i: i, 0)]
    for third in (1, 2):
        specs += [spec(half, lambda i: prompt, third), spec(half, lambda i: 0, third)]
    for third in (1, 2):
        specs += [
            spec(2 * txt_rows, lambda i: prompt, third),
            spec(2 * txt_rows, lambda i: 0, third),
        ]
    keys = 2 * half + 4 * txt_rows
    out = pl.pallas_call(
        functools.partial(attend_kernel, txt_rows, prompt),
        grid=(pairs, 2),
        out_shape=jax.ShapeDtypeStruct((2, 2, img_rows, pairs * lanes), jnp.bfloat16),
        in_specs=specs,
        out_specs=pl.BlockSpec((1, 2, img_rows, lanes), lambda j, i: (i, 0, 0, j)),
        compiler_params=pltpu.CompilerParams(vmem_limit_bytes=VMEM_BYTES),
        cost_estimate=pl.CostEstimate(
            flops=16 * 2 * half * keys * pairs * lanes,
            bytes_accessed=8 * half * pairs * lanes,
            transcendentals=2 * half * keys * pairs * 2,
        ),
    )(
        length, starts,
        img_near, img_far, img_near, img_far, img_near, img_far,
        txt_near, txt_far, txt_near, txt_far,
    )
    return out.reshape(2 * half, pairs * lanes)


def tail_kernel(*refs):
    (own_next, first_heads, outs, pieces, up_in, downs), refs = take(refs, 1, 4, 4, 8, 1, 8)
    mod, w_final, out = refs[:3]
    heads, states, wo, up, down, send, core, base, chip_send, chip, resids = refs[3:14]
    local_sem, send_sem, recv_sem = refs[14:]
    step = pl.program_id(0)
    prompt, half = step // 2, 1 - lax.rem(step, 2)
    img_rows = states.shape[2]
    two = 2 * img_rows
    cfg, req, me = (lax.axis_index(name) for name in ("cfg", "req", "seq"))
    reqs = lax.axis_size("req")
    near, far = me ^ 1, me ^ 2
    units = downs[0].shape[0]

    def remote(at, source, target, seq):
        return pltpu.make_async_remote_copy(
            src_ref=source,
            dst_ref=target,
            send_sem=send_sem.at[at],
            recv_sem=recv_sem.at[at],
            device_id=(cfg, req, seq),
            device_id_type=pl.DeviceIdType.MESH,
        )

    heads_near = remote(0, own_next[0], heads.at[1, 1], near)
    heads_far = remote(1, own_next[0], heads.at[1, 2], far)
    heads_relay = remote(2, heads.at[1, 2], heads.at[1, 3], near)
    to_core = [remote(3 + p, send.at[p], core.at[p], near) for p in range(2)]
    to_chip = [remote(5 + p, chip_send.at[p], chip.at[p], far) for p in range(2)]

    pairs = [(first_heads[r], heads.at[0, r]) for r in range(4)]
    pairs += [(pieces[4 * p + r].at[pl.ds(0, img_rows)], states.at[p, r]) for p in (0, 1) for r in range(4)]
    pairs += [(outs[r], wo.at[r]) for r in range(4)]
    early = len(pairs)
    pairs += [(own_next[0], heads.at[1, 0]), (up_in[0], up)]
    for at, shard in enumerate(downs):
        place = ((cfg ^ (at // 4)) * reqs + (req ^ (at % 4))) * units
        pairs.append((shard, down.at[pl.ds(pl.multiple_of(place, units), units)]))
    loads = [
        pltpu.make_async_copy(source, target, local_sem.at[at])
        for at, (source, target) in enumerate(pairs)
    ]

    @pl.when(step == 0)
    def _():
        barrier = pltpu.get_barrier_semaphore()
        for seq in (near, far):
            pl.semaphore_signal(
                barrier, inc=1, device_id=(cfg, req, seq), device_id_type=pl.DeviceIdType.MESH
            )
        for load in loads:
            load.start()
        pl.semaphore_wait(barrier, 2)
        heads_far.start()
        heads_near.start()
        for load in loads[:early]:
            load.wait()

    @pl.when(step == 2)
    def _():
        heads_near.wait()
        heads_relay.wait()

    proj = None
    for r in range(4):
        rows = heads[prompt, r, half ^ (r % 2)]
        if r >= 2:
            rows = jnp.concatenate([rows[img_rows:], rows[:img_rows]], axis=0)
        term = jnp.dot(rows, wo[r], preferred_element_type=jnp.float32)
        proj = term if proj is None else proj + term
    state = jnp.concatenate([states[prompt, half], states[prompt, half + 2]], axis=0)
    resid = (state.astype(jnp.float32) + mod[prompt, 2:3] * proj).astype(jnp.bfloat16)
    normed = norm_rows(resid, mod[prompt, 4:5], mod[prompt, 3:4])

    @pl.when(step == 0)
    def _():
        for load in loads[early:]:
            load.wait()

    cut = 512
    total = None
    for start in range(0, up.shape[0], cut):
        inner = across(normed, up[pl.ds(start, cut)])
        hidden = jax.nn.gelu(inner, approximate=True).astype(jnp.bfloat16)
        term = jnp.dot(hidden, down[pl.ds(start, cut)], preferred_element_type=jnp.float32)
        total = term if total is None else total + term

    for p in range(2):

        @pl.when(step == 2 * p)
        def _():
            send[p] = total.astype(jnp.bfloat16)
            to_core[p].start()

        @pl.when(step == 2 * p + 1)
        def _():
            to_core[p].wait()
            chip_send[p] = (total[img_rows:] + core[p, img_rows:].astype(jnp.float32)).astype(
                jnp.bfloat16
            )
            to_chip[p].start()
            base[p] = total[:img_rows] + core[p, :img_rows].astype(jnp.float32)
            resids[p] = resid[:img_rows]

    @pl.when(step == 0)
    def _():
        heads_far.wait()
        heads_relay.start()

    @pl.when(step == 3)
    def _():
        for p in range(2):
            to_chip[p].wait()
            mlp = base[p] + chip[p].astype(jnp.float32)
            two_sum = resids[p].astype(jnp.float32) + mod[p, 5:6] * mlp
            last = norm_rows(two_sum, mod[p, 9:10], mod[p, 8:9])
            out[p] = jnp.dot(last, w_final[...], preferred_element_type=jnp.float32)


def take(refs, *counts):
    groups = []
    for count in counts:
        groups.append(refs[:count])
        refs = refs[count:]
    return groups, refs


def tail(own_next, first_heads, outs, pieces, up, downs, parts, w_final, img_rows):
    width = parts.shape[2]
    local_width = outs[0].shape[0]
    units = up.shape[0]
    two = 2 * img_rows
    split = [rows.reshape(2, two, local_width) for rows in [own_next] + first_heads]
    vmem = pl.BlockSpec(memory_space=pltpu.VMEM)
    anywhere = pl.BlockSpec(memory_space=pl.ANY)
    bf16, f32 = jnp.bfloat16, jnp.float32
    rows = 8 * img_rows
    operands = split + outs + pieces + [up] + downs
    loads = len(operands)
    return pl.pallas_call(
        tail_kernel,
        grid=(4,),
        out_shape=jax.ShapeDtypeStruct((2, img_rows, w_final.shape[1]), f32),
        in_specs=[anywhere] * loads + [vmem, vmem],
        out_specs=vmem,
        scratch_shapes=[
            pltpu.VMEM((2, 4, 2, two, local_width), bf16),
            pltpu.VMEM((2, 4, img_rows, width), bf16),
            pltpu.VMEM((4, local_width, width), bf16),
            pltpu.VMEM((units, width), bf16),
            pltpu.VMEM((units, width), bf16),
            pltpu.VMEM((2, two, width), bf16),
            pltpu.VMEM((2, two, width), bf16),
            pltpu.VMEM((2, img_rows, width), f32),
            pltpu.VMEM((2, img_rows, width), bf16),
            pltpu.VMEM((2, img_rows, width), bf16),
            pltpu.VMEM((2, img_rows, width), bf16),
            pltpu.SemaphoreType.DMA((loads,)),
            pltpu.SemaphoreType.DMA((7,)),
            pltpu.SemaphoreType.DMA((7,)),
        ],
        compiler_params=pltpu.CompilerParams(
            collective_id=1, has_side_effects=True, vmem_limit_bytes=VMEM_BYTES
        ),
        cost_estimate=pl.CostEstimate(
            flops=2 * rows * width * (width + 2 * units),
            bytes_accessed=2 * width * (width + 2 * units) + 8 * rows * width,
            transcendentals=rows * units,
        ),
    )(*operands, parts, w_final)


def fast(
    img_state,
    txt_state,
    cond_vec,
    text_len,
    latent,
    w_mod,
    w_qkv_img,
    w_qkv_txt,
    w_attn_out,
    w_up,
    w_down,
    w_final,
):
    prompts = img_state.shape[1]
    img_rows = img_state.shape[2]
    txt_rows = txt_state.shape[2]
    width = img_state.shape[3]
    parts = modulation(cond_vec[0], w_mod)
    own = [
        after(jnp.concatenate([img_state[0, p], txt_state[0, p]], axis=0), parts)
        for p in range(prompts)
    ]
    pieces = []
    for rows in own:
        sent = after(rows, pieces[-1][2]) if pieces else rows
        pieces.append([rows, flip(rows, 1), flip(sent, 2)])
    for rows in pieces:
        rows.append(flip(rows[2], 1))
    up = lax.all_gather(after(w_up, parts), ("cfg", "req"), axis=0, tiled=True)
    first = after(w_down, parts)
    downs = [first] + [flip(first, bits, "req") for bits in (1, 2, 3)]
    downs += [flip(one, 1, "cfg") for one in downs]
    w_img = w_qkv_img.reshape(-1, width)
    w_txt = w_qkv_txt.reshape(-1, width)
    me = lax.axis_index("seq")
    starts = jnp.stack([txt_rows * (me ^ r) for r in range(4)]).astype(jnp.int32)
    near = project(
        [rows[r] for rows in pieces for r in (0, 1)],
        [p for p in range(prompts) for r in (0, 1)],
        img_rows, parts, w_img, w_txt,
    )
    outs = [w_attn_out, flip(w_attn_out, 1), flip(after(w_attn_out, pieces[-1][2]), 2)]
    outs.append(flip(outs[2], 1))
    attended = []
    for p in range(prompts):
        far = project(pieces[p][2:], [p, p], img_rows, parts, w_img, w_txt)
        attended.append(attention(p, text_len[0], starts, near, far, img_rows))
    heads = [attended[0], flip(attended[0], 1), flip(attended[0], 2)]
    heads.append(flip(heads[2], 1))
    branch_vel = tail(
        attended[1], heads, outs, pieces[0] + pieces[1], up, downs, parts, w_final, img_rows
    )
    return guide(branch_vel, latent)


def guide(branch_vel, latent):
    half_width = latent.shape[2]
    branch_index = lax.axis_index("cfg")
    own_half = lax.dynamic_slice_in_dim(branch_vel, branch_index * half_width, half_width, 2)
    other_half = lax.dynamic_slice_in_dim(
        branch_vel, (1 - branch_index) * half_width, half_width, 2
    )
    partner = partner_2(other_half.astype(jnp.bfloat16), "cfg", 0).astype(other_half.dtype)
    first = branch_index == 0
    cond_vel = jnp.where(first, own_half, partner)
    uncond_vel = jnp.where(first, partner, own_half)
    velocity = uncond_vel + 4.5 * (cond_vel - uncond_vel)
    latent_next = latent - 0.04 * velocity
    return (velocity, latent_next)


def plan(*shards):
    img_state, txt_state, w_qkv_img = shards[0], shards[1], shards[6]
    fits = (
        lax.axis_size("seq") == 4
        and lax.axis_size("req") == 4
        and lax.axis_size("cfg") == 2
        and img_state.shape[1] == 2
        and shards[9].shape[0] % 16 == 0
        and img_state.shape[2] % 128 == 0
        and txt_state.shape[2] % 16 == 0
        and w_qkv_img.shape[1] % (2 * HEAD) == 0
    )
    return fast(*shards) if fits else local(*shards)


def solution(mesh):
    placed = (
        P("cfg", "req", "seq", None),
        P("cfg", "req", "seq", None),
        P("cfg", None, None),
        P("cfg", "req"),
        P("req", "seq", "cfg"),
        P(("req", "seq"), None),
        P(None, "seq", None),
        P(None, "seq", None),
        P("seq", None),
        P(("cfg", "req", "seq"), None),
        P(("cfg", "req", "seq"), None),
        P(),
    )
    return jax.shard_map(
        plan,
        mesh=mesh,
        in_specs=placed,
        out_specs=(P("req", "seq", "cfg"), P("req", "seq", "cfg")),
        check_vma=False,
    )
```

profile of v0, /device:TPU:8, one launch (start us, length us, event | category | flops | bytes accessed | tf_op | source)
XLA Modules:
  0.0 268.3 jit_solution(5664302182755216521)
XLA Ops:
  7.2 0.0 all-gather.2.cloned.1.call-start
  7.2 10.4 %shard_map.131 = f32[16,2,960]{2,1,0:T(2,128)} custom-call(f32[8,1536]{1,0:T(8,128)} %bitcast.30, bf16[960,1536]{1,0:T(8,128)(2,1)} %weight.1), custom_call_target="tpu_custom_call" | custom-call | flops 23592960 | bytes 2949120 | tf_op jit(solution)/shard_map/pallas_call | solution.py:189
  17.6 0.9 copy.19
  18.6 0.8 reshape.25.refs_4_.refs_2_.refs_26_
  19.4 0.0 all-gather.2.cloned.1.call-update
  19.5 0.1 slice_bitcast_fusion
  19.6 1.4 pad_maximum_fusion
  21.0 1.8 collective-permute-start.2
  22.8 0.0 collective-permute-start
  22.8 0.5 collective-permute-start.1
  23.3 20.7 %collective-permute-done.2.refs_0_.refs_11_ = bf16[304,1536]{1,0:T(8,128)(2,1)S(1)} collective-permute-done((bf16[304,1536]{1,0:T(8,128)(2,1)}, bf16[304,1536]{1,0:T(8,128)(2,1)S(1)}, u32[]{:S(2)}, u32[]{:S(2)}) %collective-permute-start.2) | collective-permute-done | bytes 933920 | tf_op jit(solution)/shard_map/ppermute | solution.py:130
  44.0 1.7 collective-permute-start.3
  45.7 0.0 collective-permute-start.5
  45.7 0.8 collective-permute-start.12
  46.5 0.6 pad_add_fusion.starts
  47.1 0.0 collective-permute-done.refs_1_.refs_10_
  47.1 2.0 collective-permute-start.13
  49.1 0.0 collective-permute-done.1.refs_3_.refs_14_
  49.1 0.7 collective-permute-start.14
  49.8 11.2 %shard_map.132 = (bf16[1024,1152]{1,0:T(8,128)(2,1)}, bf16[192,1152]{1,0:T(8,128)(2,1)}) custom-call(bf16[304,1536]{1,0:T(8,128)(2,1)} %get-tuple-element.14.refs_0_.refs_9_, bf16[304,1536]{1,0:T(8,128)(2,1)} %collective-permute-done.refs_1_.refs_10_, bf16[304,1536]{1,0:T(8,128)(2,1)} %get-tuple-element.17.refs_2_.refs_13_, ...), custom_call_target="tpu_custom_call" | custom-call | flops 4303355904 | bytes 7077888 | tf_op jit(solution)/shard_map/pallas_call | solution.py:229
  61.0 17.8 %collective-permute-done.12.refs_19_ = bf16[192,1536]{1,0:T(8,128)(2,1)} collective-permute-done((bf16[192,1536]{1,0:T(8,128)(2,1)}, bf16[192,1536]{1,0:T(8,128)(2,1)}, u32[]{:S(2)}, u32[]{:S(2)}) %collective-permute-start.12) | collective-permute-done | bytes 589856 | tf_op jit(solution)/shard_map/ppermute | solution.py:130
  78.8 1.5 collective-permute-start.15
  80.3 0.0 collective-permute-done.3.refs_0_.refs_15_
  80.3 0.6 collective-permute-start.16
  80.9 0.0 collective-permute-done.5.refs_1_.refs_12_
  80.9 1.5 collective-permute-start.10
  82.3 8.2 %shard_map.135 = (bf16[512,1152]{1,0:T(8,128)(2,1)}, bf16[96,1152]{1,0:T(8,128)(2,1)}) custom-call(bf16[304,1536]{1,0:T(8,128)(2,1)} %copy-done.1, bf16[304,1536]{1,0:T(8,128)(2,1)} %copy-done.3, f32[2,10,1536]{2,1,0:T(8,128)} %reshape.25.refs_4_.refs_2_.refs_26_, bf16[1152,1536]{1,0:T(8,128)(2,1)} %bitcast.24, bf16[1152,1536]{1,0:T(8,128)(2,1)} %bitcast.27), custom_call_target="tpu_custom_call" | custom-call | flops 2151677952 | bytes 7077888 | tf_op jit(solution)/shard_map/pallas_call | solution.py:229
  90.5 0.0 collective-permute-done.13.refs_20_
  90.5 0.1 collective-permute-start.4
  90.6 0.0 copy-start.6
  90.6 18.0 %shard_map.136 = bf16[2,2,256,384]{3,2,1,0:T(8,128)(2,1)} custom-call(s32[2]{0:T(128)} %bitcast.35, s32[4]{0:T(128)} %pad_add_fusion.starts, bf16[1024,1152]{1,0:T(8,128)(2,1)} %get-tuple-element.16.qa.ka.va, bf16[512,1152]{1,0:T(8,128)(2,1)} %get-tuple-element.21.qb.kb.vb, bf16[1024,1152]{1,0:T(8,128)(2,1)} %get-tuple-element.16.qa.ka.va, ...), custom_call_target="tpu_custom_call" | custom-call | flops 7650410496 | bytes 1572864 | tf_op jit(solution)/shard_map/pallas_call | solution.py:308
  108.6 24.8 %collective-permute-done.14.refs_21_ = bf16[192,1536]{1,0:T(8,128)(2,1)S(1)} collective-permute-done((bf16[192,1536]{1,0:T(8,128)(2,1)}, bf16[192,1536]{1,0:T(8,128)(2,1)S(1)}, u32[]{:S(2)}, u32[]{:S(2)}) %collective-permute-start.14) | collective-permute-done | bytes 589856 | tf_op jit(solution)/shard_map/ppermute | solution.py:130
  133.4 0.0 collective-permute-start.7
  133.4 0.0 collective-permute-done.15.refs_22_
  133.4 1.5 collective-permute-start.17
  135.0 0.0 collective-permute-done.16.refs_23_
  135.0 0.1 collective-permute-start.9
  135.1 0.7 copy-done.13
  135.8 0.0 collective-permute-done.10.refs_7_
  135.8 0.0 collective-permute-start.11
  135.8 1.0 copy.20.refs_27_
  136.8 15.1 %collective-permute-done.7 = bf16[1024,384]{1,0:T(8,128)(2,1)} collective-permute-done((bf16[1024,384]{1,0:T(8,128)(2,1)}, bf16[1024,384]{1,0:T(8,128)(2,1)}, u32[]{:S(2)}, u32[]{:S(2)}) %collective-permute-start.7) | collective-permute-done | bytes 786464 | tf_op jit(solution)/shard_map/ppermute | solution.py:130
  151.9 0.0 collective-permute-start.6
  151.9 0.0 collective-permute-done.4.refs_1_.refs_16_
  151.9 0.5 collective-permute-start.8
  152.4 0.5 copy-done.4
  152.8 8.1 %shard_map.133 = (bf16[512,1152]{1,0:T(8,128)(2,1)}, bf16[96,1152]{1,0:T(8,128)(2,1)}) custom-call(bf16[304,1536]{1,0:T(8,128)(2,1)} %copy-done.2, bf16[304,1536]{1,0:T(8,128)(2,1)} %copy-done.4, f32[2,10,1536]{2,1,0:T(8,128)} %reshape.25.refs_4_.refs_2_.refs_26_, bf16[1152,1536]{1,0:T(8,128)(2,1)} %bitcast.25, bf16[1152,1536]{1,0:T(8,128)(2,1)} %bitcast.28), custom_call_target="tpu_custom_call" | custom-call | flops 2151677952 | bytes 7077888 | tf_op jit(solution)/shard_map/pallas_call | solution.py:229
  161.0 0.1 collective-permute-start.18
  161.1 17.9 %shard_map.134 = bf16[2,2,256,384]{3,2,1,0:T(8,128)(2,1)} custom-call(s32[2]{0:T(128)} %bitcast.36, s32[4]{0:T(128)} %pad_add_fusion.starts, bf16[1024,1152]{1,0:T(8,128)(2,1)} %get-tuple-element.16.qa.ka.va, bf16[512,1152]{1,0:T(8,128)(2,1)} %get-tuple-element.18.qb.kb.vb, bf16[1024,1152]{1,0:T(8,128)(2,1)} %get-tuple-element.16.qa.ka.va, ...), custom_call_target="tpu_custom_call" | custom-call | flops 7650410496 | bytes 1572864 | tf_op jit(solution)/shard_map/pallas_call | solution.py:308
  178.9 0.0 collective-permute-done.9.refs_6_
  178.9 0.0 collective-permute-done.6
  179.0 0.0 collective-permute-done.11.refs_8_
  179.0 0.0 all-gather.2.cloned.1.call-done.refs_17_
  179.0 0.9 copy-done.9
  180.0 0.1 copy-done.14
  180.0 0.4 copy-done.8
  180.5 72.3 %shard_map.137 = f32[2,256,64]{2,1,0:T(8,128)} custom-call(bf16[2,512,384]{2,1,0:T(8,128)(2,1)} %bitcast.37, bf16[2,512,384]{2,1,0:T(8,128)(2,1)} %bitcast.33, bf16[2,512,384]{2,1,0:T(8,128)(2,1)} %bitcast.16.refs_2_, bf16[2,512,384]{2,1,0:T(8,128)(2,1)} %bitcast.17.refs_3_, bf16[2,512,384]{2,1,0:T(8,128)(2,1)} %bitcast.34, bf16[384,1536]{1,0:T(8,128)(2,1)} %refs_5_.1, ...), custom_call_target="tpu_custom_call" | custom-call | flops 28991029248 | bytes 39321600 | tf_op jit(solution)/shard_map/pallas_call | solution.py:467
  252.8 1.1 dynamic-slice_convert_fusion
  253.9 1.4 collective-permute-start.19
  255.3 0.1 copy.21
  255.4 3.5 %collective-permute-done.19 = bf16[2,256,32]{2,1,0:T(8,128)(2,1)S(1)} collective-permute-done((bf16[2,256,32]{2,1,0:T(8,128)(2,1)S(1)}, bf16[2,256,32]{2,1,0:T(8,128)(2,1)S(1)}, u32[]{:S(2)}, u32[]{:S(2)}) %collective-permute-start.19) | collective-permute-done | bytes 32800 | tf_op jit(solution)/shard_map/ppermute | solution.py:15
  258.9 1.1 multiply_subtract_fusion
  260.0 0.7 copy.22
  260.7 0.7 copy.23
  (28 shorter events, 0.1 us)
Async XLA Ops:
  7.2 171.8 %all-gather.2.cloned.1.call-start = ((), (), s32[]{:S(2)}) async-start(), calls=%async_computation | async-start | bytes 5308416 | tf_op jit(solution)/shard_map/all_gather | solution.py:529
  7.2 12.2 %copy-start.5 = (bf16[1,2,48,1536]{3,2,1,0:T(8,128)(2,1)S(1)}, bf16[1,2,48,1536]{3,2,1,0:T(8,128)(2,1)}, u32[]{:S(2)}) copy-start(bf16[1,2,48,1536]{3,2,1,0:T(8,128)(2,1)} %param.13) | copy-start | bytes 884740
  7.2 12.2 %copy-start = (bf16[1,2,256,1536]{3,2,1,0:T(8,128)(2,1)S(1)}, bf16[1,2,256,1536]{3,2,1,0:T(8,128)(2,1)}, u32[]{:S(2)}) copy-start(bf16[1,2,256,1536]{3,2,1,0:T(8,128)(2,1)} %param.12) | copy-start | bytes 4718596
  21.0 23.0 %collective-permute-start.2 = (bf16[304,1536]{1,0:T(8,128)(2,1)}, bf16[304,1536]{1,0:T(8,128)(2,1)S(1)}, u32[]{:S(2)}, u32[]{:S(2)}) collective-permute-start(bf16[304,1536]{1,0:T(8,128)(2,1)} %get-tuple-element.14.refs_0_.refs_9_), channel_id=1, source_target_pairs={{0,2},{1,3},{2,0},{3,1},{4,6},{5,7},{6,4},{7,5},{8,10},{9,11},{10,... | collective-permute-start | bytes 2801672 | tf_op jit(solution)/shard_map/ppermute | solution.py:130
  22.8 24.3 %collective-permute-start = (bf16[304,1536]{1,0:T(8,128)(2,1)}, bf16[304,1536]{1,0:T(8,128)(2,1)}, u32[]{:S(2)}, u32[]{:S(2)}) collective-permute-start(bf16[304,1536]{1,0:T(8,128)(2,1)} %get-tuple-element.14.refs_0_.refs_9_), channel_id=1, source_target_pairs={{0,1},{1,0},{2,3},{3,2},{4,5},{5,4},{6,7},{7,6},{8,9},{9,8},{10,11... | collective-permute-start | bytes 2801672 | tf_op jit(solution)/shard_map/ppermute | solution.py:130
  22.8 26.3 %collective-permute-start.1 = (bf16[304,1536]{1,0:T(8,128)(2,1)}, bf16[304,1536]{1,0:T(8,128)(2,1)}, u32[]{:S(2)}, u32[]{:S(2)}) collective-permute-start(bf16[304,1536]{1,0:T(8,128)(2,1)} %get-tuple-element.17.refs_2_.refs_13_), channel_id=1, source_target_pairs={{0,1},{1,0},{2,3},{3,2},{4,5},{5,4},{6,7},{7,6},{8,9},{9,8},{10,11... | collective-permute-start | bytes 2801672 | tf_op jit(solution)/shard_map/ppermute | solution.py:130
  44.0 17.0 %copy-start.1 = (bf16[304,1536]{1,0:T(8,128)(2,1)}, bf16[304,1536]{1,0:T(8,128)(2,1)S(1)}, u32[]{:S(2)}) copy-start(bf16[304,1536]{1,0:T(8,128)(2,1)S(1)} %collective-permute-done.2.refs_0_.refs_11_) | copy-start | bytes 2801668
  44.0 36.3 %collective-permute-start.3 = (bf16[304,1536]{1,0:T(8,128)(2,1)}, bf16[304,1536]{1,0:T(8,128)(2,1)S(1)}, u32[]{:S(2)}, u32[]{:S(2)}) collective-permute-start(bf16[304,1536]{1,0:T(8,128)(2,1)} %get-tuple-element.17.refs_2_.refs_13_), channel_id=1, source_target_pairs={{0,2},{1,3},{2,0},{3,1},{4,6},{5,7},{6,4},{7,5},{8,10},{9,11},{10,... | collective-permute-start | bytes 2801672 | tf_op jit(solution)/shard_map/ppermute | solution.py:130
  45.7 35.1 %collective-permute-start.5 = (bf16[304,1536]{1,0:T(8,128)(2,1)S(1)}, bf16[304,1536]{1,0:T(8,128)(2,1)S(1)}, u32[]{:S(2)}, u32[]{:S(2)}) collective-permute-start(bf16[304,1536]{1,0:T(8,128)(2,1)S(1)} %collective-permute-done.2.refs_0_.refs_11_), channel_id=1, source_target_pairs={{0,1},{1,0},{2,3},{3,2},{4,5},{5,4},{6,7},{7,6},{8,9},{9,8},{10,11... | collective-permute-start | bytes 2801672 | tf_op jit(solution)/shard_map/ppermute | solution.py:130
  45.7 33.1 %collective-permute-start.12 = (bf16[192,1536]{1,0:T(8,128)(2,1)}, bf16[192,1536]{1,0:T(8,128)(2,1)}, u32[]{:S(2)}, u32[]{:S(2)}) collective-permute-start(bf16[192,1536]{1,0:T(8,128)(2,1)} %refs_18_), channel_id=1, source_target_pairs={{0,4},{4,0},{8,12},{12,8},{1,5},{5,1},{9,13},{13,9},{2,6},{6,2},{1... | collective-permute-start | bytes 1769480 | tf_op jit(solution)/shard_map/ppermute | solution.py:130
  47.1 43.4 %collective-permute-start.13 = (bf16[192,1536]{1,0:T(8,128)(2,1)}, bf16[192,1536]{1,0:T(8,128)(2,1)}, u32[]{:S(2)}, u32[]{:S(2)}) collective-permute-start(bf16[192,1536]{1,0:T(8,128)(2,1)} %refs_18_), channel_id=1, source_target_pairs={{0,8},{4,12},{8,0},{12,4},{1,9},{5,13},{9,1},{13,5},{2,10},{6,14},... | collective-permute-start | bytes 1769480 | tf_op jit(solution)/shard_map/ppermute | solution.py:130
  49.1 84.3 %collective-permute-start.14 = (bf16[192,1536]{1,0:T(8,128)(2,1)}, bf16[192,1536]{1,0:T(8,128)(2,1)S(1)}, u32[]{:S(2)}, u32[]{:S(2)}) collective-permute-start(bf16[192,1536]{1,0:T(8,128)(2,1)} %refs_18_), channel_id=1, source_target_pairs={{0,12},{4,8},{8,4},{12,0},{1,13},{5,9},{9,5},{13,1},{2,14},{6,10},... | collective-permute-start | bytes 1769480 | tf_op jit(solution)/shard_map/ppermute | solution.py:130
  78.8 54.6 %collective-permute-start.15 = (bf16[192,1536]{1,0:T(8,128)(2,1)}, bf16[192,1536]{1,0:T(8,128)(2,1)S(1)}, u32[]{:S(2)}, u32[]{:S(2)}) collective-permute-start(bf16[192,1536]{1,0:T(8,128)(2,1)} %refs_18_), channel_id=1, source_target_pairs={{0,16},{16,0},{1,17},{17,1},{2,18},{18,2},{3,19},{19,3},{4,20},{20... | collective-permute-start | bytes 1769480 | tf_op jit(solution)/shard_map/ppermute | solution.py:130
  80.3 10.3 %copy-start.2 = (bf16[304,1536]{1,0:T(8,128)(2,1)}, bf16[304,1536]{1,0:T(8,128)(2,1)S(1)}, u32[]{:S(2)}) copy-start(bf16[304,1536]{1,0:T(8,128)(2,1)S(1)} %collective-permute-done.3.refs_0_.refs_15_) | copy-start | bytes 2801668
  80.3 54.7 %collective-permute-start.16 = (bf16[192,1536]{1,0:T(8,128)(2,1)}, bf16[192,1536]{1,0:T(8,128)(2,1)S(1)}, u32[]{:S(2)}, u32[]{:S(2)}) collective-permute-start(bf16[192,1536]{1,0:T(8,128)(2,1)} %collective-permute-done.12.refs_19_), channel_id=1, source_target_pairs={{0,16},{16,0},{1,17},{17,1},{2,18},{18,2},{3,19},{19,3},{4,20},{20... | collective-permute-start | bytes 1769480 | tf_op jit(solution)/shard_map/ppermute | solution.py:130
  80.9 1.5 copy-start.3
  80.9 55.0 %collective-permute-start.10 = (bf16[384,1536]{1,0:T(8,128)(2,1)}, bf16[384,1536]{1,0:T(8,128)(2,1)}, u32[]{:S(2)}, u32[]{:S(2)}) collective-permute-start(bf16[384,1536]{1,0:T(8,128)(2,1)} %refs_5_.1), channel_id=1, source_target_pairs={{0,2},{1,3},{2,0},{3,1},{4,6},{5,7},{6,4},{7,5},{8,10},{9,11},{10,... | collective-permute-start | bytes 3538952 | tf_op jit(solution)/shard_map/ppermute | solution.py:130
  90.5 61.3 %collective-permute-start.4 = (bf16[304,1536]{1,0:T(8,128)(2,1)S(1)}, bf16[304,1536]{1,0:T(8,128)(2,1)S(1)}, u32[]{:S(2)}, u32[]{:S(2)}) collective-permute-start(bf16[304,1536]{1,0:T(8,128)(2,1)S(1)} %collective-permute-done.3.refs_0_.refs_15_), channel_id=1, source_target_pairs={{0,1},{1,0},{2,3},{3,2},{4,5},{5,4},{6,7},{7,6},{8,9},{9,8},{10,11... | collective-permute-start | bytes 2801672 | tf_op jit(solution)/shard_map/ppermute | solution.py:130
  90.6 45.2 %copy-start.6 = (bf16[1536,64]{0,1:T(8,128)(2,1)S(1)}, bf16[1536,64]{0,1:T(8,128)(2,1)}, u32[]{:S(2)}) copy-start(bf16[1536,64]{0,1:T(8,128)(2,1)} %param.23) | copy-start | bytes 589828
  133.4 1.6 copy-start.10
  133.4 18.4 %collective-permute-start.7 = (bf16[1024,384]{1,0:T(8,128)(2,1)}, bf16[1024,384]{1,0:T(8,128)(2,1)}, u32[]{:S(2)}, u32[]{:S(2)}) collective-permute-start(bf16[1024,384]{1,0:T(8,128)(2,1)} %bitcast.31), channel_id=1, source_target_pairs={{0,2},{1,3},{2,0},{3,1},{4,6},{5,7},{6,4},{7,5},{8,10},{9,11},{10,... | collective-permute-start | bytes 2359304 | tf_op jit(solution)/shard_map/ppermute | solution.py:130
  133.4 1.6 copy-start.12
  133.4 27.5 %collective-permute-start.17 = (bf16[192,1536]{1,0:T(8,128)(2,1)}, bf16[192,1536]{1,0:T(8,128)(2,1)}, u32[]{:S(2)}, u32[]{:S(2)}) collective-permute-start(bf16[192,1536]{1,0:T(8,128)(2,1)} %collective-permute-done.13.refs_20_), channel_id=1, source_target_pairs={{0,16},{16,0},{1,17},{17,1},{2,18},{18,2},{3,19},{19,3},{4,20},{20... | collective-permute-start | bytes 1769480 | tf_op jit(solution)/shard_map/ppermute | solution.py:130
  135.0 0.8 copy-start.13
  135.0 43.9 %collective-permute-start.9 = (bf16[384,1536]{1,0:T(8,128)(2,1)}, bf16[384,1536]{1,0:T(8,128)(2,1)S(1)}, u32[]{:S(2)}, u32[]{:S(2)}) collective-permute-start(bf16[384,1536]{1,0:T(8,128)(2,1)} %refs_5_.1), channel_id=1, source_target_pairs={{0,1},{1,0},{2,3},{3,2},{4,5},{5,4},{6,7},{7,6},{8,9},{9,8},{10,11... | collective-permute-start | bytes 3538952 | tf_op jit(solution)/shard_map/ppermute | solution.py:130
  135.8 43.2 %collective-permute-start.11 = (bf16[384,1536]{1,0:T(8,128)(2,1)}, bf16[384,1536]{1,0:T(8,128)(2,1)}, u32[]{:S(2)}, u32[]{:S(2)}) collective-permute-start(bf16[384,1536]{1,0:T(8,128)(2,1)} %collective-permute-done.10.refs_7_), channel_id=1, source_target_pairs={{0,1},{1,0},{2,3},{3,2},{4,5},{5,4},{6,7},{7,6},{8,9},{9,8},{10,11... | collective-permute-start | bytes 3538952 | tf_op jit(solution)/shard_map/ppermute | solution.py:130
  136.8 24.2 %copy-start.11 = (bf16[192,1536]{1,0:T(8,128)(2,1)S(1)}, bf16[192,1536]{1,0:T(8,128)(2,1)}, u32[]{:S(2)}) copy-start(bf16[192,1536]{1,0:T(8,128)(2,1)} %copy-done.10) | copy-start | bytes 1769476
  151.9 27.1 %collective-permute-start.6 = (bf16[1024,384]{1,0:T(8,128)(2,1)}, bf16[1024,384]{1,0:T(8,128)(2,1)}, u32[]{:S(2)}, u32[]{:S(2)}) collective-permute-start(bf16[1024,384]{1,0:T(8,128)(2,1)} %bitcast.32), channel_id=1, source_target_pairs={{0,1},{1,0},{2,3},{3,2},{4,5},{5,4},{6,7},{7,6},{8,9},{9,8},{10,11... | collective-permute-start | bytes 2359304 | tf_op jit(solution)/shard_map/ppermute | solution.py:130
  151.9 1.0 copy-start.4
  151.9 27.1 %collective-permute-start.8 = (bf16[1024,384]{1,0:T(8,128)(2,1)}, bf16[1024,384]{1,0:T(8,128)(2,1)S(1)}, u32[]{:S(2)}, u32[]{:S(2)}) collective-permute-start(bf16[1024,384]{1,0:T(8,128)(2,1)} %collective-permute-done.7), channel_id=1, source_target_pairs={{0,1},{1,0},{2,3},{3,2},{4,5},{5,4},{6,7},{7,6},{8,9},{9,8},{10,11... | collective-permute-start | bytes 2359304 | tf_op jit(solution)/shard_map/ppermute | solution.py:130
  161.0 17.9 %collective-permute-start.18 = (bf16[192,1536]{1,0:T(8,128)(2,1)S(1)}, bf16[192,1536]{1,0:T(8,128)(2,1)S(1)}, u32[]{:S(2)}, u32[]{:S(2)}) collective-permute-start(bf16[192,1536]{1,0:T(8,128)(2,1)S(1)} %copy-done.11), channel_id=1, source_target_pairs={{0,16},{16,0},{1,17},{17,1},{2,18},{18,2},{3,19},{19,3},{4,20},{20... | collective-permute-start | bytes 1769480 | tf_op jit(solution)/shard_map/ppermute | solution.py:130
  178.9 1.1 copy-start.14
  178.9 1.5 copy-start.8
  179.0 1.0 copy-start.9
  180.5 74.8 %copy-start.7 = (f32[2,256,32]{1,2,0:T(8,128)S(1)}, f32[2,256,32]{1,2,0:T(8,128)}, u32[]{:S(2)}) copy-start(f32[2,256,32]{1,2,0:T(8,128)} %param.16) | copy-start | bytes 196612
  253.9 5.0 %collective-permute-start.19 = (bf16[2,256,32]{2,1,0:T(8,128)(2,1)S(1)}, bf16[2,256,32]{2,1,0:T(8,128)(2,1)S(1)}, u32[]{:S(2)}, u32[]{:S(2)}) collective-permute-start(bf16[2,256,32]{2,1,0:T(8,128)(2,1)S(1)} %dynamic-slice_convert_fusion), channel_id=1, source_target_pairs={{0,16},{16,0},{1,17},{17,1},{2,18},{18,2},{3,19},{19,3},{4,20},{20... | collective-permute-start | bytes 98312 | tf_op jit(solution)/shard_map/ppermute | solution.py:15
Sparse Core Ops, SparseCore 0:
  19.5 118.9 all-gather.1
where the time goes:
time: 269 us; the launch traced here: 268 us
  Pallas kernels  146 us (54%)
  waiting for transfers between devices  82 us (30%)
  starting transfers between devices  14.8 us (6%)
  between operations  14.3 us (5%)
  local copies, waits for them, and re-layouts  8.18 us (3%)
  other arithmetic  3.08 us (1%)
    ppermute x19, waiting for transfers between devices, flip(): lax.ppermute(shard, axis, [(i, i ^ bits) for i in range(lax.axis_size(axi...  78.4 us
    pallas_call x1, Pallas kernels, tail(): pl.pallas_call(tail_kernel, grid=(4,), out_shape=jax.ShapeDtypeStruct((2,...  72.3 us
    pallas_call x2, Pallas kernels, attention(): pl.pallas_call(functools.partial(attend_kernel, txt_rows, prompt), grid=(...  35.8 us
    pallas_call x3, Pallas kernels, project(): pl.pallas_call(functools.partial(qkv_kernel, owners, img_rows, txt_rows),...  27.5 us
    ppermute x19, starting transfers between devices, flip(): lax.ppermute(shard, axis, [(i, i ^ bits) for i in range(lax.axis_size(axi...  13.3 us
    pallas_call x1, Pallas kernels, modulation(): pl.pallas_call(mod_kernel, out_shape=jax.ShapeDtypeStruct((group, prompts...  10.4 us
  transfers between devices with their start and end apart: 21, of which 5 were waited for; matrix products, arithmetic and copies ran while one was open for 1% of the time, Pallas kernels for 24%

commit v1 on v0

--- a/solution.py
+++ b/solution.py
@@ -200,9 +200,6 @@
         compiler_params=pltpu.CompilerParams(
             collective_id=0, has_side_effects=True, vmem_limit_bytes=VMEM_BYTES
         ),
-        cost_estimate=pl.CostEstimate(
-            flops=2 * cond.size * columns, bytes_accessed=2 * weight.size, transcendentals=0
-        ),
     )(cond, weight)
     return jnp.swapaxes(got, 0, 1).reshape(prompts, 10, -1)
 
@@ -236,9 +233,6 @@
         out_specs=(pl.BlockSpec(memory_space=pltpu.VMEM),) * 2,
         scratch_shapes=[pltpu.VMEM((count * txt_rows, width), jnp.bfloat16)],
         compiler_params=pltpu.CompilerParams(vmem_limit_bytes=VMEM_BYTES),
-        cost_estimate=pl.CostEstimate(
-            flops=2 * rows * width * out, bytes_accessed=4 * out * width, transcendentals=0
-        ),
     )(*pieces, parts, w_img, w_txt)
 
 
@@ -312,11 +306,6 @@
         in_specs=specs,
         out_specs=pl.BlockSpec((1, 2, img_rows, lanes), lambda j, i: (i, 0, 0, j)),
         compiler_params=pltpu.CompilerParams(vmem_limit_bytes=VMEM_BYTES),
-        cost_estimate=pl.CostEstimate(
-            flops=16 * 2 * half * keys * pairs * lanes,
-            bytes_accessed=8 * half * pairs * lanes,
-            transcendentals=2 * half * keys * pairs * 2,
-        ),
     )(
         length, starts,
         img_near, img_far, img_near, img_far, img_near, img_far,
@@ -325,15 +314,63 @@
     return out.reshape(2 * half, pairs * lanes)
 
 
+def attn_out_kernel(prompt, img_rows, *refs):
+    (heads, outs, pieces), refs = take(refs, 4, 4, 4)
+    mod, normed, resid_out, state = refs
+    step = pl.program_id(0)
+    for half in range(2):
+
+        @pl.when(step == 1 - half)
+        def _():
+            state[:img_rows] = pieces[half][:img_rows]
+            state[img_rows:] = pieces[half + 2][:img_rows]
+
+    proj = None
+    for r in range(4):
+        rows = heads[r][...]
+        if r >= 2:
+            rows = jnp.concatenate([rows[img_rows:], rows[:img_rows]], axis=0)
+        term = jnp.dot(rows, outs[r][...], preferred_element_type=jnp.float32)
+        proj = term if proj is None else proj + term
+    resid = (state[...].astype(jnp.float32) + mod[prompt, 2:3] * proj).astype(jnp.bfloat16)
+    normed[...] = norm_rows(resid, mod[prompt, 4:5], mod[prompt, 3:4])
+    resid_out[...] = resid[:img_rows]
+
+
+def attn_out(prompt, heads, outs, pieces, parts, img_rows):
+    width = parts.shape[2]
+    local_width = heads[0].shape[1]
+    two = 2 * img_rows
+
+    def spec(apart):
+        return pl.BlockSpec((two, local_width), lambda t: ((1 - t) ^ (apart % 2), 0))
+
+    vmem = pl.BlockSpec(memory_space=pltpu.VMEM)
+    return pl.pallas_call(
+        functools.partial(attn_out_kernel, prompt, img_rows),
+        grid=(2,),
+        out_shape=(
+            jax.ShapeDtypeStruct((2 * two, width), jnp.bfloat16),
+            jax.ShapeDtypeStruct((img_rows, width), jnp.bfloat16),
+        ),
+        in_specs=[spec(r) for r in range(4)] + [vmem] * 9,
+        out_specs=(
+            pl.BlockSpec((two, width), lambda t: (1 - t, 0)),
+            pl.BlockSpec((img_rows, width), lambda t: (0, 0)),
+        ),
+        scratch_shapes=[pltpu.VMEM((two, width), jnp.bfloat16)],
+        compiler_params=pltpu.CompilerParams(vmem_limit_bytes=40 * 1024 * 1024),
+    )(*heads, *outs, *pieces, parts)
+
+
 def tail_kernel(*refs):
-    (own_next, first_heads, outs, pieces, up_in, downs), refs = take(refs, 1, 4, 4, 8, 1, 8)
+    (normed_in, resid_in, up_in, downs), refs = take(refs, 2, 2, 1, 8)
     mod, w_final, out = refs[:3]
-    heads, states, wo, up, down, send, core, base, chip_send, chip, resids = refs[3:14]
-    local_sem, send_sem, recv_sem = refs[14:]
+    normeds, resids, up, down, send, core, base, chip_send, chip = refs[3:12]
+    local_sem, send_sem, recv_sem = refs[12:]
     step = pl.program_id(0)
     prompt, half = step // 2, 1 - lax.rem(step, 2)
-    img_rows = states.shape[2]
-    two = 2 * img_rows
+    img_rows = resids.shape[1]
     cfg, req, me = (lax.axis_index(name) for name in ("cfg", "req", "seq"))
     reqs = lax.axis_size("req")
     near, far = me ^ 1, me ^ 2
@@ -349,20 +386,16 @@
             device_id_type=pl.DeviceIdType.MESH,
         )
 
-    heads_near = remote(0, own_next[0], heads.at[1, 1], near)
-    heads_far = remote(1, own_next[0], heads.at[1, 2], far)
-    heads_relay = remote(2, heads.at[1, 2], heads.at[1, 3], near)
-    to_core = [remote(3 + p, send.at[p], core.at[p], near) for p in range(2)]
-    to_chip = [remote(5 + p, chip_send.at[p], chip.at[p], far) for p in range(2)]
-
-    pairs = [(first_heads[r], heads.at[0, r]) for r in range(4)]
-    pairs += [(pieces[4 * p + r].at[pl.ds(0, img_rows)], states.at[p, r]) for p in (0, 1) for r in range(4)]
-    pairs += [(outs[r], wo.at[r]) for r in range(4)]
-    early = len(pairs)
-    pairs += [(own_next[0], heads.at[1, 0]), (up_in[0], up)]
+    to_core = [remote(p, send.at[p], core.at[p], near) for p in range(2)]
+    to_chip = [remote(2 + p, chip_send.at[p], chip.at[p], far) for p in range(2)]
+
+    pairs = [(normed_in[0], normeds.at[0]), (up_in[0], up)]
     for at, shard in enumerate(downs):
         place = ((cfg ^ (at // 4)) * reqs + (req ^ (at % 4))) * units
         pairs.append((shard, down.at[pl.ds(pl.multiple_of(place, units), units)]))
+    early = len(pairs)
+    pairs += [(normed_in[1], normeds.at[1])]
+    pairs += [(resid_in[p], resids.at[p]) for p in range(2)]
     loads = [
         pltpu.make_async_copy(source, target, local_sem.at[at])
         for at, (source, target) in enumerate(pairs)
@@ -378,32 +411,15 @@
         for load in loads:
             load.start()
         pl.semaphore_wait(barrier, 2)
-        heads_far.start()
-        heads_near.start()
         for load in loads[:early]:
             load.wait()
 
-    @pl.when(step == 2)
-    def _():
-        heads_near.wait()
-        heads_relay.wait()
-
-    proj = None
-    for r in range(4):
-        rows = heads[prompt, r, half ^ (r % 2)]
-        if r >= 2:
-            rows = jnp.concatenate([rows[img_rows:], rows[:img_rows]], axis=0)
-        term = jnp.dot(rows, wo[r], preferred_element_type=jnp.float32)
-        proj = term if proj is None else proj + term
-    state = jnp.concatenate([states[prompt, half], states[prompt, half + 2]], axis=0)
-    resid = (state.astype(jnp.float32) + mod[prompt, 2:3] * proj).astype(jnp.bfloat16)
-    normed = norm_rows(resid, mod[prompt, 4:5], mod[prompt, 3:4])
-
-    @pl.when(step == 0)
+    @pl.when(step == 1)
     def _():
         for load in loads[early:]:
             load.wait()
 
+    normed = normeds[prompt, half]
     cut = 512
     total = None
     for start in range(0, up.shape[0], cut):
@@ -427,12 +443,6 @@
             )
             to_chip[p].start()
             base[p] = total[:img_rows] + core[p, :img_rows].astype(jnp.float32)
-            resids[p] = resid[:img_rows]
-
-    @pl.when(step == 0)
-    def _():
-        heads_far.wait()
-        heads_relay.start()
 
     @pl.when(step == 3)
     def _():
@@ -452,17 +462,17 @@
     return groups, refs
 
 
-def tail(own_next, first_heads, outs, pieces, up, downs, parts, w_final, img_rows):
+def tail(normed, resids, up, downs, parts, w_final):
     width = parts.shape[2]
-    local_width = outs[0].shape[0]
+    img_rows = resids[0].shape[0]
     units = up.shape[0]
     two = 2 * img_rows
-    split = [rows.reshape(2, two, local_width) for rows in [own_next] + first_heads]
+    split = [rows.reshape(2, two, width) for rows in normed]
     vmem = pl.BlockSpec(memory_space=pltpu.VMEM)
     anywhere = pl.BlockSpec(memory_space=pl.ANY)
     bf16, f32 = jnp.bfloat16, jnp.float32
     rows = 8 * img_rows
-    operands = split + outs + pieces + [up] + downs
+    operands = split + resids + [up] + downs
     loads = len(operands)
     return pl.pallas_call(
         tail_kernel,
@@ -471,9 +481,8 @@
         in_specs=[anywhere] * loads + [vmem, vmem],
         out_specs=vmem,
         scratch_shapes=[
-            pltpu.VMEM((2, 4, 2, two, local_width), bf16),
-            pltpu.VMEM((2, 4, img_rows, width), bf16),
-            pltpu.VMEM((4, local_width, width), bf16),
+            pltpu.VMEM((2, 2, two, width), bf16),
+            pltpu.VMEM((2, img_rows, width), bf16),
             pltpu.VMEM((units, width), bf16),
             pltpu.VMEM((units, width), bf16),
             pltpu.VMEM((2, two, width), bf16),
@@ -481,18 +490,12 @@
             pltpu.VMEM((2, img_rows, width), f32),
             pltpu.VMEM((2, img_rows, width), bf16),
             pltpu.VMEM((2, img_rows, width), bf16),
-            pltpu.VMEM((2, img_rows, width), bf16),
             pltpu.SemaphoreType.DMA((loads,)),
-            pltpu.SemaphoreType.DMA((7,)),
-            pltpu.SemaphoreType.DMA((7,)),
+            pltpu.SemaphoreType.DMA((4,)),
+            pltpu.SemaphoreType.DMA((4,)),
         ],
         compiler_params=pltpu.CompilerParams(
             collective_id=1, has_side_effects=True, vmem_limit_bytes=VMEM_BYTES
-        ),
-        cost_estimate=pl.CostEstimate(
-            flops=2 * rows * width * (width + 2 * units),
-            bytes_accessed=2 * width * (width + 2 * units) + 8 * rows * width,
-            transcendentals=rows * units,
         ),
     )(*operands, parts, w_final)
 
@@ -520,36 +523,42 @@
         after(jnp.concatenate([img_state[0, p], txt_state[0, p]], axis=0), parts)
         for p in range(prompts)
     ]
-    pieces = []
-    for rows in own:
-        sent = after(rows, pieces[-1][2]) if pieces else rows
-        pieces.append([rows, flip(rows, 1), flip(sent, 2)])
-    for rows in pieces:
-        rows.append(flip(rows[2], 1))
     up = lax.all_gather(after(w_up, parts), ("cfg", "req"), axis=0, tiled=True)
     first = after(w_down, parts)
     downs = [first] + [flip(first, bits, "req") for bits in (1, 2, 3)]
-    downs += [flip(one, 1, "cfg") for one in downs]
     w_img = w_qkv_img.reshape(-1, width)
     w_txt = w_qkv_txt.reshape(-1, width)
     me = lax.axis_index("seq")
     starts = jnp.stack([txt_rows * (me ^ r) for r in range(4)]).astype(jnp.int32)
+    pieces = [[rows, flip(rows, 1)] for rows in own]
     near = project(
         [rows[r] for rows in pieces for r in (0, 1)],
         [p for p in range(prompts) for r in (0, 1)],
         img_rows, parts, w_img, w_txt,
     )
-    outs = [w_attn_out, flip(w_attn_out, 1), flip(after(w_attn_out, pieces[-1][2]), 2)]
-    outs.append(flip(outs[2], 1))
+    for p, rows in enumerate(pieces):
+        rows.append(flip(after(rows[0], near[0]) if p else rows[0], 2))
+    pieces[0].append(flip(pieces[0][2], 1))
     attended = []
     for p in range(prompts):
+        if p == 0:
+            starts = after(starts, downs[1:3])
+        else:
+            starts = after(starts, downs[3])
+            pieces[p].append(flip(after(pieces[p][2], attended[0]), 1))
         far = project(pieces[p][2:], [p, p], img_rows, parts, w_img, w_txt)
         attended.append(attention(p, text_len[0], starts, near, far, img_rows))
-    heads = [attended[0], flip(attended[0], 1), flip(attended[0], 2)]
-    heads.append(flip(heads[2], 1))
-    branch_vel = tail(
-        attended[1], heads, outs, pieces[0] + pieces[1], up, downs, parts, w_final, img_rows
-    )
+    downs += [flip(after(one, attended[0]) if at else one, 1, "cfg") for at, one in enumerate(downs)]
+    outs = [w_attn_out, flip(w_attn_out, 1), flip(after(w_attn_out, attended[0]), 2)]
+    outs.append(flip(outs[2], 1))
+    normed, resids = [], []
+    for p in range(prompts):
+        heads = [after(attended[p], attended[-1]) if p == 0 else attended[p], flip(attended[p], 1), flip(attended[p], 2)]
+        heads.append(flip(heads[2], 1))
+        rows, resid = attn_out(p, heads, outs, pieces[p], parts, img_rows)
+        normed.append(rows)
+        resids.append(resid)
+    branch_vel = tail(normed, resids, up, downs, parts, w_final)
     return guide(branch_vel, latent)
 
 

time: 269 us -> 314 us (1.17)
  waiting for transfers between devices: 82 us -> 102 us
  local copies, waits for them, and re-layouts: 8.18 us -> 25.5 us
  Pallas kernels: 146 us -> 152 us
    pallas_call x0 -> x2, Pallas kernels: none -> 23.6 us  [attn_out(): pl.pallas_call(functools.partial(attn_out_kernel, prompt, img_rows), grid...]
    ppermute x19 -> x22, waiting for transfers between devices: 78.4 us -> 98.7 us  [flip(): lax.ppermute(shard, axis, [(i, i ^ bits) for i in range(lax.axis_size(axi...]
    pallas_call x1, Pallas kernels: 72.3 us -> 54.9 us  [tail(): pl.pallas_call(tail_kernel, grid=(4,), out_shape=jax.ShapeDtypeStruct((2,...]
    unnamed x34 -> x88, local copies, waits for them, and re-layouts: 5.25 us -> 22.5 us
    ppermute x19 -> x22, starting transfers between devices: 13.3 us -> 16 us  [flip(): lax.ppermute(shard, axis, [(i, i ^ bits) for i in range(lax.axis_size(axi...]
  transfers between devices with their start and end apart: 21 -> 24, of which waited for: 5 -> 8; matrix products, arithmetic and copies ran while one was open for 1% -> 1% of each run, Pallas kernels for 24% -> 28%
where the time goes in v1:
time: 314 us
  Pallas kernels  152 us (48%)
  waiting for transfers between devices  102 us (32%)
  local copies, waits for them, and re-layouts  25.5 us (8%)
  starting transfers between devices  17.6 us (6%)
  between operations  14.3 us (5%)
    ppermute x22, waiting for transfers between devices, flip(): lax.ppermute(shard, axis, [(i, i ^ bits) for i in range(lax.axis_size(axi...  98.7 us
    pallas_call x1, Pallas kernels, tail(): pl.pallas_call(tail_kernel, grid=(4,), out_shape=jax.ShapeDtypeStruct((2,...  54.9 us
    pallas_call x2, Pallas kernels, attention(): pl.pallas_call(functools.partial(attend_kernel, txt_rows, prompt), grid=(...  36 us
    pallas_call x3, Pallas kernels, project(): pl.pallas_call(functools.partial(qkv_kernel, owners, img_rows, txt_rows),...  27.4 us
    pallas_call x2, Pallas kernels, attn_out(): pl.pallas_call(functools.partial(attn_out_kernel, prompt, img_rows), grid...  23.6 us
    unnamed x88, local copies, waits for them, and re-layouts  22.5 us
    ppermute x22, starting transfers between devices, flip(): lax.ppermute(shard, axis, [(i, i ^ bits) for i in range(lax.axis_size(axi...  16 us
    pallas_call x1, Pallas kernels, modulation(): pl.pallas_call(mod_kernel, out_shape=jax.ShapeDtypeStruct((group, prompts...  10.4 us
  transfers between devices with their start and end apart: 24, of which 8 were waited for; matrix products, arithmetic and copies ran while one was open for 1% of the time, Pallas kernels for 28%

profile of v1, /device:TPU:8, one launch (start us, length us, event | category | flops | bytes accessed | tf_op | source)
XLA Modules:
  0.0 313.7 jit_solution(5177541402595975325)
XLA Ops:
  7.2 10.4 %shard_map.131 = f32[16,2,960]{2,1,0:T(2,128)} custom-call(f32[8,1536]{1,0:T(8,128)} %bitcast.36, bf16[960,1536]{1,0:T(8,128)(2,1)} %weight.1), custom_call_target="tpu_custom_call" | custom-call | tf_op jit(solution)/shard_map/pallas_call | solution.py:189
  17.6 0.9 copy.19
  18.6 0.8 reshape.25.refs_4_.refs_2_.refs_12_.refs_13_
  19.5 0.1 slice_bitcast_fusion
  19.6 0.1 pad_maximum_fusion
  19.7 1.9 collective-permute-start.4
  21.6 0.5 collective-permute-start.2
  22.1 20.5 %collective-permute-done.4.refs_0_.refs_10_ = bf16[304,1536]{1,0:T(8,128)(2,1)S(1)} collective-permute-done((bf16[304,1536]{1,0:T(8,128)(2,1)S(1)}, bf16[304,1536]{1,0:T(8,128)(2,1)S(1)}, u32[]{:S(2)}, u32[]{:S(2)}) %collective-permute-start.4) | collective-permute-done | bytes 933920 | tf_op jit(solution)/shard_map/ppermute | solution.py:130
  42.6 0.8 collective-permute-start
  43.4 2.0 collective-permute-start.1
  45.5 1.0 copy-done.18
  46.5 0.3 copy-done.20
  46.8 11.1 %shard_map.132 = (bf16[1024,1152]{1,0:T(8,128)(2,1)}, bf16[192,1152]{1,0:T(8,128)(2,1)}) custom-call(bf16[304,1536]{1,0:T(8,128)(2,1)} %copy-done.3, bf16[304,1536]{1,0:T(8,128)(2,1)} %copy-done.20, bf16[304,1536]{1,0:T(8,128)(2,1)} %copy-done.1, bf16[304,1536]{1,0:T(8,128)(2,1)} %copy-done.18, f32[2,10,1536]{2,1,0:T(8,128)} %reshape.25.refs_4_.refs_2_.refs_12_.refs_13_, ...), custom_call_target="tpu_custom_call" | custom-call | tf_op jit(solution)/shard_map/pallas_call | solution.py:226
  57.9 1.7 collective-permute-start.7
  59.6 0.7 pad_add_fusion.starts
  60.3 16.8 %collective-permute-done.refs_6_ = bf16[192,1536]{1,0:T(8,128)(2,1)S(1)} collective-permute-done((bf16[192,1536]{1,0:T(8,128)(2,1)S(1)}, bf16[192,1536]{1,0:T(8,128)(2,1)S(1)}, u32[]{:S(2)}, u32[]{:S(2)}) %collective-permute-start) | collective-permute-done | bytes 589856 | tf_op jit(solution)/shard_map/ppermute | solution.py:130
  77.2 3.2 %collective-permute-done.1.refs_7_ = bf16[192,1536]{1,0:T(8,128)(2,1)} collective-permute-done((bf16[192,1536]{1,0:T(8,128)(2,1)S(1)}, bf16[192,1536]{1,0:T(8,128)(2,1)}, u32[]{:S(2)}, u32[]{:S(2)}) %collective-permute-start.1) | collective-permute-done | bytes 589856 | tf_op jit(solution)/shard_map/ppermute | solution.py:130
  80.3 8.2 %shard_map.133 = (bf16[512,1152]{1,0:T(8,128)(2,1)}, bf16[96,1152]{1,0:T(8,128)(2,1)}) custom-call(bf16[304,1536]{1,0:T(8,128)(2,1)} %copy-done.12, bf16[304,1536]{1,0:T(8,128)(2,1)} %collective-permute-done.5.refs_1_.refs_11_, f32[2,10,1536]{2,1,0:T(8,128)} %reshape.25.refs_4_.refs_2_.refs_12_.refs_13_, bf16[1152,1536]{1,0:T(8,128)(2,1)} %bitcast.28, ...), custom_call_target="tpu_custom_call" | custom-call | tf_op jit(solution)/shard_map/pallas_call | solution.py:226
  88.5 18.1 %shard_map.134 = bf16[2,2,256,384]{3,2,1,0:T(8,128)(2,1)} custom-call(s32[2]{0:T(128)} %bitcast.37, s32[4]{0:T(128)} %pad_add_fusion.starts, bf16[1024,1152]{1,0:T(8,128)(2,1)} %get-tuple-element.29.qa.ka.va, bf16[512,1152]{1,0:T(8,128)(2,1)} %get-tuple-element.30.qb.kb.vb, bf16[1024,1152]{1,0:T(8,128)(2,1)} %get-tuple-element.29.qa.ka.va, ...), custom_call_target="tpu_custom_call" | custom-call | tf_op jit(solution)/shard_map/pallas_call | solution.py:302
  106.6 1.5 collective-permute-start.13
  108.1 0.5 collective-permute-start.8
  108.7 0.2 collective-permute-start.6
  108.9 0.6 collective-permute-start.10
  109.4 26.1 %collective-permute-done.13.refs_6_ = bf16[384,1536]{1,0:T(8,128)(2,1)S(1)} collective-permute-done((bf16[384,1536]{1,0:T(8,128)(2,1)S(1)}, bf16[384,1536]{1,0:T(8,128)(2,1)S(1)}, u32[]{:S(2)}, u32[]{:S(2)}) %collective-permute-start.13) | collective-permute-done | bytes 1179680 | tf_op jit(solution)/shard_map/ppermute | solution.py:130
  135.5 5.3 %collective-permute-done.6.refs_8_ = bf16[192,1536]{1,0:T(8,128)(2,1)S(1)} collective-permute-done((bf16[192,1536]{1,0:T(8,128)(2,1)S(1)}, bf16[192,1536]{1,0:T(8,128)(2,1)S(1)}, u32[]{:S(2)}, u32[]{:S(2)}) %collective-permute-start.6) | collective-permute-done | bytes 589856 | tf_op jit(solution)/shard_map/ppermute | solution.py:130
  140.9 0.8 copy-done.39
  141.7 1.0 copy-done.16
  142.7 8.1 %shard_map.135 = (bf16[512,1152]{1,0:T(8,128)(2,1)}, bf16[96,1152]{1,0:T(8,128)(2,1)}) custom-call(bf16[304,1536]{1,0:T(8,128)(2,1)} %copy-done.14, bf16[304,1536]{1,0:T(8,128)(2,1)} %copy-done.16, f32[2,10,1536]{2,1,0:T(8,128)} %reshape.25.refs_4_.refs_2_.refs_12_.refs_13_, bf16[1152,1536]{1,0:T(8,128)(2,1)} %bitcast.29, bf16[1152,1536]{1,0:T(8,128)(2,1)} %bitcast.32), custom_call_target="tpu_custom_call" | custom-call | tf_op jit(solution)/shard_map/pallas_call | solution.py:226
  150.8 17.9 %shard_map.136 = bf16[2,2,256,384]{3,2,1,0:T(8,128)(2,1)} custom-call(s32[2]{0:T(128)} %bitcast.38, s32[4]{0:T(128)} %pad_add_fusion.starts, bf16[1024,1152]{1,0:T(8,128)(2,1)} %get-tuple-element.29.qa.ka.va, bf16[512,1152]{1,0:T(8,128)(2,1)} %get-tuple-element.36.qb.kb.vb, bf16[1024,1152]{1,0:T(8,128)(2,1)} %get-tuple-element.29.qa.ka.va, ...), custom_call_target="tpu_custom_call" | custom-call | tf_op jit(solution)/shard_map/pallas_call | solution.py:302
  168.7 1.6 collective-permute-start.16
  170.3 0.5 collective-permute-start.11
  170.8 0.9 copy-done.27
  171.7 1.0 copy-done.6
  172.7 0.1 collective-permute-start.15
  172.8 15.6 %collective-permute-done.16.refs_2_ = bf16[1024,384]{1,0:T(8,128)(2,1)} collective-permute-done((bf16[1024,384]{1,0:T(8,128)(2,1)}, bf16[1024,384]{1,0:T(8,128)(2,1)}, u32[]{:S(2)}, u32[]{:S(2)}) %collective-permute-start.16) | collective-permute-done | bytes 786464 | tf_op jit(solution)/shard_map/ppermute | solution.py:130
  188.4 0.9 copy-done.31
  189.3 1.5 collective-permute-start.18
  190.8 0.9 copy-done.33
  191.7 0.5 collective-permute-start.19
  192.3 0.9 copy-done.29
  193.2 1.5 collective-permute-start.20
  194.7 1.0 copy-done.9
  195.7 0.5 collective-permute-start.21
  196.2 1.9 copy.20.refs_14_
  198.1 1.3 copy-done.7
  199.3 1.3 copy-done.10
  200.6 1.2 copy-done.13
  201.8 1.2 copy-done.21
  203.0 1.1 copy-done.23
  204.1 1.1 copy-done.28
  205.3 1.1 copy-done.32
  206.4 1.1 copy-done.34
  207.6 11.9 %shard_map.137 = (bf16[1024,1536]{1,0:T(8,128)(2,1)}, bf16[256,1536]{1,0:T(8,128)(2,1)S(1)}) custom-call(bf16[1024,384]{1,0:T(8,128)(2,1)S(1)} %bitcast.23, bf16[1024,384]{1,0:T(8,128)(2,1)S(1)} %copy-done.32, bf16[1024,384]{1,0:T(8,128)(2,1)S(1)} %copy-done.28, bf16[1024,384]{1,0:T(8,128)(2,1)S(1)} %copy-done.34, bf16[384,1536]{1,0:T(8,128)(2,1)S(1)} %copy-done.5, ...), custom_call_target="tpu_custom_call" | custom-call | tf_op jit(solution)/shard_map/pallas_call | solution.py:349
  219.6 11.7 %shard_map.138 = (bf16[1024,1536]{1,0:T(8,128)(2,1)}, bf16[256,1536]{1,0:T(8,128)(2,1)S(1)}) custom-call(bf16[1024,384]{1,0:T(8,128)(2,1)S(1)} %bitcast.26, bf16[1024,384]{1,0:T(8,128)(2,1)S(1)} %copy-done.30, bf16[1024,384]{1,0:T(8,128)(2,1)} %collective-permute-done.16.refs_2_, bf16[1024,384]{1,0:T(8,128)(2,1)} %collective-permute-done.17.refs_3_, ...), custom_call_target="tpu_custom_call" | custom-call | tf_op jit(solution)/shard_map/pallas_call | solution.py:349
  231.2 0.9 copy-done.26
  232.1 11.2 %collective-permute-done.21.refs_12_ = bf16[192,1536]{1,0:T(8,128)(2,1)} collective-permute-done((bf16[192,1536]{1,0:T(8,128)(2,1)}, bf16[192,1536]{1,0:T(8,128)(2,1)}, u32[]{:S(2)}, u32[]{:S(2)}) %collective-permute-start.21) | collective-permute-done | bytes 589856 | tf_op jit(solution)/shard_map/ppermute | solution.py:130
  243.3 54.9 %shard_map.139 = f32[2,256,64]{2,1,0:T(8,128)} custom-call(bf16[2,512,1536]{2,1,0:T(8,128)(2,1)} %bitcast.33, bf16[2,512,1536]{2,1,0:T(8,128)(2,1)} %bitcast.34, bf16[256,1536]{1,0:T(8,128)(2,1)} %copy-done.25, bf16[256,1536]{1,0:T(8,128)(2,1)} %copy-done.26, bf16[1536,1536]{1,0:T(8,128)(2,1)} %all-gather.2.cloned.1.call-done.refs_4_, ...), custom_call_target="tpu_custom_call" | custom-call | tf_op jit(solution)/shard_map/pallas_call | solution.py:477
  298.2 1.1 dynamic-slice_convert_fusion
  299.3 1.5 collective-permute-start.22
  300.8 0.1 copy.21
  300.9 3.4 %collective-permute-done.22 = bf16[2,256,32]{2,1,0:T(8,128)(2,1)S(1)} collective-permute-done((bf16[2,256,32]{2,1,0:T(8,128)(2,1)S(1)}, bf16[2,256,32]{2,1,0:T(8,128)(2,1)S(1)}, u32[]{:S(2)}, u32[]{:S(2)}) %collective-permute-start.22) | collective-permute-done | bytes 32800 | tf_op jit(solution)/shard_map/ppermute | solution.py:15
  304.3 1.1 multiply_subtract_fusion
  305.4 0.7 copy.22
  306.1 0.7 copy.23
  (90 shorter events, 0.3 us)
Async XLA Ops:
  7.2 236.1 %all-gather.2.cloned.1.call-start = ((), (), s32[]{:S(2)}) async-start(), calls=%async_computation | async-start | bytes 5308416 | tf_op jit(solution)/shard_map/all_gather | solution.py:526
  7.2 12.2 %copy-start.40 = (bf16[1,2,48,1536]{3,2,1,0:T(8,128)(2,1)S(1)}, bf16[1,2,48,1536]{3,2,1,0:T(8,128)(2,1)}, u32[]{:S(2)}) copy-start(bf16[1,2,48,1536]{3,2,1,0:T(8,128)(2,1)} %param.13) | copy-start | bytes 884740
  7.2 12.2 %copy-start.35 = (bf16[1,2,256,1536]{3,2,1,0:T(8,128)(2,1)S(1)}, bf16[1,2,256,1536]{3,2,1,0:T(8,128)(2,1)}, u32[]{:S(2)}) copy-start(bf16[1,2,256,1536]{3,2,1,0:T(8,128)(2,1)} %param.12) | copy-start | bytes 4718596
  19.6 23.0 %copy-start.36 = (bf16[192,1536]{1,0:T(8,128)(2,1)S(1)}, bf16[192,1536]{1,0:T(8,128)(2,1)}, u32[]{:S(2)}) copy-start(bf16[192,1536]{1,0:T(8,128)(2,1)} %refs_5_) | copy-start | bytes 1769476
  19.7 25.8 %copy-start.1 = (bf16[304,1536]{1,0:T(8,128)(2,1)}, bf16[304,1536]{1,0:T(8,128)(2,1)S(1)}, u32[]{:S(2)}) copy-start(bf16[304,1536]{1,0:T(8,128)(2,1)S(1)} %get-tuple-element.34.refs_2_.refs_8_) | copy-start | bytes 2801668
  19.7 25.8 %copy-start.3 = (bf16[304,1536]{1,0:T(8,128)(2,1)}, bf16[304,1536]{1,0:T(8,128)(2,1)S(1)}, u32[]{:S(2)}) copy-start(bf16[304,1536]{1,0:T(8,128)(2,1)S(1)} %get-tuple-element.27.refs_0_.refs_8_) | copy-start | bytes 2801668
  19.7 22.9 %collective-permute-start.4 = (bf16[304,1536]{1,0:T(8,128)(2,1)S(1)}, bf16[304,1536]{1,0:T(8,128)(2,1)S(1)}, u32[]{:S(2)}, u32[]{:S(2)}) collective-permute-start(bf16[304,1536]{1,0:T(8,128)(2,1)S(1)} %get-tuple-element.27.refs_0_.refs_8_), channel_id=1, source_target_pairs={{0,2},{1,3},{2,0},{3,1},{4,6},{5,7},{6,4},{7,5},{8,10},{9,11},{10,... | collective-permute-start | bytes 2801672 | tf_op jit(solution)/shard_map/ppermute | solution.py:130
  21.6 23.9 %collective-permute-start.3 = (bf16[304,1536]{1,0:T(8,128)(2,1)S(1)}, bf16[304,1536]{1,0:T(8,128)(2,1)S(1)}, u32[]{:S(2)}, u32[]{:S(2)}) collective-permute-start(bf16[304,1536]{1,0:T(8,128)(2,1)S(1)} %get-tuple-element.34.refs_2_.refs_8_), channel_id=1, source_target_pairs={{0,1},{1,0},{2,3},{3,2},{4,5},{5,4},{6,7},{7,6},{8,9},{9,8},{10,11... | collective-permute-start | bytes 2801672 | tf_op jit(solution)/shard_map/ppermute | solution.py:130
  21.6 23.9 %collective-permute-start.2 = (bf16[304,1536]{1,0:T(8,128)(2,1)S(1)}, bf16[304,1536]{1,0:T(8,128)(2,1)S(1)}, u32[]{:S(2)}, u32[]{:S(2)}) collective-permute-start(bf16[304,1536]{1,0:T(8,128)(2,1)S(1)} %get-tuple-element.27.refs_0_.refs_8_), channel_id=1, source_target_pairs={{0,1},{1,0},{2,3},{3,2},{4,5},{5,4},{6,7},{7,6},{8,9},{9,8},{10,11... | collective-permute-start | bytes 2801672 | tf_op jit(solution)/shard_map/ppermute | solution.py:130
  42.6 15.3 %copy-start.12 = (bf16[304,1536]{1,0:T(8,128)(2,1)}, bf16[304,1536]{1,0:T(8,128)(2,1)S(1)}, u32[]{:S(2)}) copy-start(bf16[304,1536]{1,0:T(8,128)(2,1)S(1)} %collective-permute-done.4.refs_0_.refs_10_) | copy-start | bytes 2801668
  42.6 37.7 %collective-permute-start.5 = (bf16[304,1536]{1,0:T(8,128)(2,1)S(1)}, bf16[304,1536]{1,0:T(8,128)(2,1)}, u32[]{:S(2)}, u32[]{:S(2)}) collective-permute-start(bf16[304,1536]{1,0:T(8,128)(2,1)S(1)} %collective-permute-done.4.refs_0_.refs_10_), channel_id=1, source_target_pairs={{0,1},{1,0},{2,3},{3,2},{4,5},{5,4},{6,7},{7,6},{8,9},{9,8},{10,11... | collective-permute-start | bytes 2801672 | tf_op jit(solution)/shard_map/ppermute | solution.py:130
  42.6 34.6 %collective-permute-start = (bf16[192,1536]{1,0:T(8,128)(2,1)S(1)}, bf16[192,1536]{1,0:T(8,128)(2,1)S(1)}, u32[]{:S(2)}, u32[]{:S(2)}) collective-permute-start(bf16[192,1536]{1,0:T(8,128)(2,1)S(1)} %copy-done.36), channel_id=1, source_target_pairs={{0,4},{4,0},{8,12},{12,8},{1,5},{5,1},{9,13},{13,9},{2,6},{6,2},{1... | collective-permute-start | bytes 1769480 | tf_op jit(solution)/shard_map/ppermute | solution.py:130
  43.4 36.9 %collective-permute-start.1 = (bf16[192,1536]{1,0:T(8,128)(2,1)S(1)}, bf16[192,1536]{1,0:T(8,128)(2,1)}, u32[]{:S(2)}, u32[]{:S(2)}) collective-permute-start(bf16[192,1536]{1,0:T(8,128)(2,1)S(1)} %copy-done.36), channel_id=1, source_target_pairs={{0,8},{4,12},{8,0},{12,4},{1,9},{5,13},{9,1},{13,5},{2,10},{6,14},... | collective-permute-start | bytes 1769480 | tf_op jit(solution)/shard_map/ppermute | solution.py:130
  45.5 1.0 copy-start.18
  45.5 1.3 copy-start.20
  57.9 50.2 %collective-permute-start.7 = (bf16[304,1536]{1,0:T(8,128)(2,1)}, bf16[304,1536]{1,0:T(8,128)(2,1)S(1)}, u32[]{:S(2)}, u32[]{:S(2)}) collective-permute-start(bf16[304,1536]{1,0:T(8,128)(2,1)} %copy-done.1), channel_id=1, source_target_pairs={{0,2},{1,3},{2,0},{3,1},{4,6},{5,7},{6,4},{7,5},{8,10},{9,11},{10,... | collective-permute-start | bytes 2801672 | tf_op jit(solution)/shard_map/ppermute | solution.py:130
  77.2 11.3 %copy-start.38 = (bf16[192,1536]{1,0:T(8,128)(2,1)}, bf16[192,1536]{1,0:T(8,128)(2,1)S(1)}, u32[]{:S(2)}) copy-start(bf16[192,1536]{1,0:T(8,128)(2,1)S(1)} %collective-permute-done.refs_6_) | copy-start | bytes 1769476
  88.5 18.1 %copy-start.5 = (bf16[384,1536]{1,0:T(8,128)(2,1)S(1)}, bf16[384,1536]{1,0:T(8,128)(2,1)}, u32[]{:S(2)}) copy-start(bf16[384,1536]{1,0:T(8,128)(2,1)} %refs_4_.3) | copy-start | bytes 3538948
  88.5 20.2 %copy-start.37 = (bf16[192,1536]{1,0:T(8,128)(2,1)S(1)}, bf16[192,1536]{1,0:T(8,128)(2,1)}, u32[]{:S(2)}) copy-start(bf16[192,1536]{1,0:T(8,128)(2,1)} %refs_5_) | copy-start | bytes 1769476
  106.6 28.9 %collective-permute-start.13 = (bf16[384,1536]{1,0:T(8,128)(2,1)S(1)}, bf16[384,1536]{1,0:T(8,128)(2,1)S(1)}, u32[]{:S(2)}, u32[]{:S(2)}) collective-permute-start(bf16[384,1536]{1,0:T(8,128)(2,1)S(1)} %copy-done.5), channel_id=1, source_target_pairs={{0,2},{1,3},{2,0},{3,1},{4,6},{5,7},{6,4},{7,5},{8,10},{9,11},{10,... | collective-permute-start | bytes 3538952 | tf_op jit(solution)/shard_map/ppermute | solution.py:130
  108.1 63.6 %collective-permute-start.12 = (bf16[384,1536]{1,0:T(8,128)(2,1)S(1)}, bf16[384,1536]{1,0:T(8,128)(2,1)S(1)}, u32[]{:S(2)}, u32[]{:S(2)}) collective-permute-start(bf16[384,1536]{1,0:T(8,128)(2,1)S(1)} %copy-done.5), channel_id=1, source_target_pairs={{0,1},{1,0},{2,3},{3,2},{4,5},{5,4},{6,7},{7,6},{8,9},{9,8},{10,11... | collective-permute-start | bytes 3538952 | tf_op jit(solution)/shard_map/ppermute | solution.py:130
  108.1 33.5 %copy-start.14 = (bf16[304,1536]{1,0:T(8,128)(2,1)}, bf16[304,1536]{1,0:T(8,128)(2,1)S(1)}, u32[]{:S(2)}) copy-start(bf16[304,1536]{1,0:T(8,128)(2,1)S(1)} %collective-permute-done.7.refs_0_.refs_10_) | copy-start | bytes 2801668
  108.1 33.5 %collective-permute-start.8 = (bf16[304,1536]{1,0:T(8,128)(2,1)S(1)}, bf16[304,1536]{1,0:T(8,128)(2,1)S(1)}, u32[]{:S(2)}, u32[]{:S(2)}) collective-permute-start(bf16[304,1536]{1,0:T(8,128)(2,1)S(1)} %collective-permute-done.7.refs_0_.refs_10_), channel_id=1, source_target_pairs={{0,1},{1,0},{2,3},{3,2},{4,5},{5,4},{6,7},{7,6},{8,9},{9,8},{10,11... | collective-permute-start | bytes 2801672 | tf_op jit(solution)/shard_map/ppermute | solution.py:130
  108.7 32.2 %collective-permute-start.6 = (bf16[192,1536]{1,0:T(8,128)(2,1)S(1)}, bf16[192,1536]{1,0:T(8,128)(2,1)S(1)}, u32[]{:S(2)}, u32[]{:S(2)}) collective-permute-start(bf16[192,1536]{1,0:T(8,128)(2,1)S(1)} %copy-done.37), channel_id=1, source_target_pairs={{0,12},{4,8},{8,4},{12,0},{1,13},{5,9},{9,5},{13,1},{2,14},{6,10},... | collective-permute-start | bytes 1769480 | tf_op jit(solution)/shard_map/ppermute | solution.py:130
  108.9 61.4 %collective-permute-start.10 = (bf16[1024,384]{1,0:T(8,128)(2,1)}, bf16[1024,384]{1,0:T(8,128)(2,1)S(1)}, u32[]{:S(2)}, u32[]{:S(2)}) collective-permute-start(bf16[1024,384]{1,0:T(8,128)(2,1)} %bitcast.21), channel_id=1, source_target_pairs={{0,2},{1,3},{2,0},{3,1},{4,6},{5,7},{6,4},{7,5},{8,10},{9,11},{10,... | collective-permute-start | bytes 2359304 | tf_op jit(solution)/shard_map/ppermute | solution.py:130
  135.5 59.1 %collective-permute-start.14 = (bf16[384,1536]{1,0:T(8,128)(2,1)S(1)}, bf16[384,1536]{1,0:T(8,128)(2,1)S(1)}, u32[]{:S(2)}, u32[]{:S(2)}) collective-permute-start(bf16[384,1536]{1,0:T(8,128)(2,1)S(1)} %collective-permute-done.13.refs_6_), channel_id=1, source_target_pairs={{0,1},{1,0},{2,3},{3,2},{4,5},{5,4},{6,7},{7,6},{8,9},{9,8},{10,11... | collective-permute-start | bytes 3538952 | tf_op jit(solution)/shard_map/ppermute | solution.py:130
  141.7 1.0 copy-start.16
  150.8 19.5 %copy-start.22 = (bf16[2,2,256,384]{3,2,1,0:T(8,128)(2,1)S(1)}, bf16[2,2,256,384]{3,2,1,0:T(8,128)(2,1)}, u32[]{:S(2)}) copy-start(bf16[2,2,256,384]{3,2,1,0:T(8,128)(2,1)} %shard_map.134) | copy-start | bytes 2359300
  150.8 47.3 %copy-start = (f32[2,10,1536]{2,1,0:T(8,128)S(1)}, f32[2,10,1536]{2,1,0:T(8,128)}, u32[]{:S(2)}) copy-start(f32[2,10,1536]{2,1,0:T(8,128)} %reshape.25.refs_4_.refs_2_.refs_12_.refs_13_) | copy-start | bytes 368644
  150.8 47.3 %copy-start.4 = (bf16[304,1536]{1,0:T(8,128)(2,1)S(1)}, bf16[304,1536]{1,0:T(8,128)(2,1)}, u32[]{:S(2)}) copy-start(bf16[304,1536]{1,0:T(8,128)(2,1)} %copy-done.3) | copy-start | bytes 2801668
  168.7 19.7 %collective-permute-start.16 = (bf16[1024,384]{1,0:T(8,128)(2,1)}, bf16[1024,384]{1,0:T(8,128)(2,1)}, u32[]{:S(2)}, u32[]{:S(2)}) collective-permute-start(bf16[1024,384]{1,0:T(8,128)(2,1)} %bitcast.24), channel_id=1, source_target_pairs={{0,2},{1,3},{2,0},{3,1},{4,6},{5,7},{6,4},{7,5},{8,10},{9,11},{10,... | collective-permute-start | bytes 2359304 | tf_op jit(solution)/shard_map/ppermute | solution.py:130
  170.3 18.1 %collective-permute-start.9 = (bf16[1024,384]{1,0:T(8,128)(2,1)S(1)}, bf16[1024,384]{1,0:T(8,128)(2,1)S(1)}, u32[]{:S(2)}, u32[]{:S(2)}) collective-permute-start(bf16[1024,384]{1,0:T(8,128)(2,1)S(1)} %bitcast.22), channel_id=1, source_target_pairs={{0,1},{1,0},{2,3},{3,2},{4,5},{5,4},{6,7},{7,6},{8,9},{9,8},{10,11... | collective-permute-start | bytes 2359304 | tf_op jit(solution)/shard_map/ppermute | solution.py:130
  170.3 20.5 %collective-permute-start.11 = (bf16[1024,384]{1,0:T(8,128)(2,1)S(1)}, bf16[1024,384]{1,0:T(8,128)(2,1)S(1)}, u32[]{:S(2)}, u32[]{:S(2)}) collective-permute-start(bf16[1024,384]{1,0:T(8,128)(2,1)S(1)} %collective-permute-done.10.refs_2_), channel_id=1, source_target_pairs={{0,1},{1,0},{2,3},{3,2},{4,5},{5,4},{6,7},{7,6},{8,9},{9,8},{10,11... | collective-permute-start | bytes 2359304 | tf_op jit(solution)/shard_map/ppermute | solution.py:130
  171.7 1.0 copy-start.6
  172.7 19.5 %collective-permute-start.15 = (bf16[1024,384]{1,0:T(8,128)(2,1)}, bf16[1024,384]{1,0:T(8,128)(2,1)S(1)}, u32[]{:S(2)}, u32[]{:S(2)}) collective-permute-start(bf16[1024,384]{1,0:T(8,128)(2,1)} %bitcast.25), channel_id=1, source_target_pairs={{0,1},{1,0},{2,3},{3,2},{4,5},{5,4},{6,7},{7,6},{8,9},{9,8},{10,11... | collective-permute-start | bytes 2359304 | tf_op jit(solution)/shard_map/ppermute | solution.py:130
  188.4 31.1 %collective-permute-start.17 = (bf16[1024,384]{1,0:T(8,128)(2,1)}, bf16[1024,384]{1,0:T(8,128)(2,1)}, u32[]{:S(2)}, u32[]{:S(2)}) collective-permute-start(bf16[1024,384]{1,0:T(8,128)(2,1)} %collective-permute-done.16.refs_2_), channel_id=1, source_target_pairs={{0,1},{1,0},{2,3},{3,2},{4,5},{5,4},{6,7},{7,6},{8,9},{9,8},{10,11... | collective-permute-start | bytes 2359304 | tf_op jit(solution)/shard_map/ppermute | solution.py:130
  188.4 0.9 copy-start.31
  189.3 42.8 %collective-permute-start.18 = (bf16[192,1536]{1,0:T(8,128)(2,1)}, bf16[192,1536]{1,0:T(8,128)(2,1)}, u32[]{:S(2)}, u32[]{:S(2)}) collective-permute-start(bf16[192,1536]{1,0:T(8,128)(2,1)} %refs_5_), channel_id=1, source_target_pairs={{0,16},{16,0},{1,17},{17,1},{2,18},{18,2},{3,19},{19,3},{4,20},{20... | collective-permute-start | bytes 1769480 | tf_op jit(solution)/shard_map/ppermute | solution.py:130
  190.8 0.9 copy-start.33
  191.7 40.4 %collective-permute-start.19 = (bf16[192,1536]{1,0:T(8,128)(2,1)}, bf16[192,1536]{1,0:T(8,128)(2,1)}, u32[]{:S(2)}, u32[]{:S(2)}) collective-permute-start(bf16[192,1536]{1,0:T(8,128)(2,1)} %copy-done.38), channel_id=1, source_target_pairs={{0,16},{16,0},{1,17},{17,1},{2,18},{18,2},{3,19},{19,3},{4,20},{20... | collective-permute-start | bytes 1769480 | tf_op jit(solution)/shard_map/ppermute | solution.py:130
  192.3 0.9 copy-start.29
  193.2 39.0 %collective-permute-start.20 = (bf16[192,1536]{1,0:T(8,128)(2,1)}, bf16[192,1536]{1,0:T(8,128)(2,1)}, u32[]{:S(2)}, u32[]{:S(2)}) collective-permute-start(bf16[192,1536]{1,0:T(8,128)(2,1)} %collective-permute-done.1.refs_7_), channel_id=1, source_target_pairs={{0,16},{16,0},{1,17},{17,1},{2,18},{18,2},{3,19},{19,3},{4,20},{20... | collective-permute-start | bytes 1769480 | tf_op jit(solution)/shard_map/ppermute | solution.py:130
  194.7 1.0 copy-start.9
  195.7 47.6 %collective-permute-start.21 = (bf16[192,1536]{1,0:T(8,128)(2,1)}, bf16[192,1536]{1,0:T(8,128)(2,1)}, u32[]{:S(2)}, u32[]{:S(2)}) collective-permute-start(bf16[192,1536]{1,0:T(8,128)(2,1)} %copy-done.39), channel_id=1, source_target_pairs={{0,16},{16,0},{1,17},{17,1},{2,18},{18,2},{3,19},{19,3},{4,20},{20... | collective-permute-start | bytes 1769480 | tf_op jit(solution)/shard_map/ppermute | solution.py:130
  198.1 1.3 copy-start.7
  199.3 1.3 copy-start.10
  200.6 1.2 copy-start.13
  201.8 1.2 copy-start.21
  203.0 1.1 copy-start.23
  204.1 1.1 copy-start.28
  205.3 1.1 copy-start.32
  206.4 1.1 copy-start.34
  207.5 12.0 %copy-start.2 = (bf16[304,1536]{1,0:T(8,128)(2,1)S(1)}, bf16[304,1536]{1,0:T(8,128)(2,1)}, u32[]{:S(2)}) copy-start(bf16[304,1536]{1,0:T(8,128)(2,1)} %copy-done.1) | copy-start | bytes 2801668
  207.5 12.0 %copy-start.8 = (bf16[384,1536]{1,0:T(8,128)(2,1)S(1)}, bf16[384,1536]{1,0:T(8,128)(2,1)}, u32[]{:S(2)}) copy-start(bf16[384,1536]{1,0:T(8,128)(2,1)} %copy-done.6) | copy-start | bytes 3538948
  207.5 12.0 %copy-start.11 = (bf16[384,1536]{1,0:T(8,128)(2,1)S(1)}, bf16[384,1536]{1,0:T(8,128)(2,1)}, u32[]{:S(2)}) copy-start(bf16[384,1536]{1,0:T(8,128)(2,1)} %copy-done.9) | copy-start | bytes 3538948
  207.5 12.0 %copy-start.15 = (bf16[304,1536]{1,0:T(8,128)(2,1)S(1)}, bf16[304,1536]{1,0:T(8,128)(2,1)}, u32[]{:S(2)}) copy-start(bf16[304,1536]{1,0:T(8,128)(2,1)} %copy-done.14) | copy-start | bytes 2801668
  207.5 12.0 %copy-start.17 = (bf16[304,1536]{1,0:T(8,128)(2,1)S(1)}, bf16[304,1536]{1,0:T(8,128)(2,1)}, u32[]{:S(2)}) copy-start(bf16[304,1536]{1,0:T(8,128)(2,1)} %copy-done.16) | copy-start | bytes 2801668
  207.5 12.0 %copy-start.19 = (bf16[304,1536]{1,0:T(8,128)(2,1)S(1)}, bf16[304,1536]{1,0:T(8,128)(2,1)}, u32[]{:S(2)}) copy-start(bf16[304,1536]{1,0:T(8,128)(2,1)} %copy-done.18) | copy-start | bytes 2801668
  207.6 12.0 %copy-start.24 = (bf16[2,2,256,384]{3,2,1,0:T(8,128)(2,1)S(1)}, bf16[2,2,256,384]{3,2,1,0:T(8,128)(2,1)}, u32[]{:S(2)}) copy-start(bf16[2,2,256,384]{3,2,1,0:T(8,128)(2,1)} %shard_map.136) | copy-start | bytes 2359300
  207.6 12.0 %copy-start.30 = (bf16[1024,384]{1,0:T(8,128)(2,1)S(1)}, bf16[1024,384]{1,0:T(8,128)(2,1)}, u32[]{:S(2)}) copy-start(bf16[1024,384]{1,0:T(8,128)(2,1)} %copy-done.29) | copy-start | bytes 2359300
  219.5 11.7 %copy-start.25 = (bf16[256,1536]{1,0:T(8,128)(2,1)}, bf16[256,1536]{1,0:T(8,128)(2,1)S(1)}, u32[]{:S(2)}) copy-start(bf16[256,1536]{1,0:T(8,128)(2,1)S(1)} %get-tuple-element.42.refs_2_) | copy-start | bytes 2359300
  231.2 0.9 copy-start.26
  243.3 57.5 %copy-start.41 = (f32[2,256,32]{1,2,0:T(8,128)S(1)}, f32[2,256,32]{1,2,0:T(8,128)}, u32[]{:S(2)}) copy-start(f32[2,256,32]{1,2,0:T(8,128)} %param.16) | copy-start | bytes 196612
  299.3 5.0 %collective-permute-start.22 = (bf16[2,256,32]{2,1,0:T(8,128)(2,1)S(1)}, bf16[2,256,32]{2,1,0:T(8,128)(2,1)S(1)}, u32[]{:S(2)}, u32[]{:S(2)}) collective-permute-start(bf16[2,256,32]{2,1,0:T(8,128)(2,1)S(1)} %dynamic-slice_convert_fusion), channel_id=1, source_target_pairs={{0,16},{16,0},{1,17},{17,1},{2,18},{18,2},{3,19},{19,3},{4,20},{20... | collective-permute-start | bytes 98312 | tf_op jit(solution)/shard_map/ppermute | solution.py:15
  (2 other events, 1.7 us)
Sparse Core Ops, SparseCore 0:
  19.5 107.3 all-gather.1
